TPU v7x, 32 devices: a whole 2x2x4 slice. The times are simulated.
32 devices in a mesh: gx: 4 (over x, core), gy: 4 (over z), gz: 2 (over y).
Axes of the slice: x: 2, y: 2, z: 4, core: 2. Of those that a mesh axis runs over, the one named last changes fastest.
Arguments:
- fields: float32 [4, 32, 128, 256], P(None, 'gx', 'gy', 'gz'), may hold values from -6 to 6
- viscosity: float32 [32, 128, 256], P('gx', 'gy', 'gz'), may hold values from 0.02 to 0.6
- samples: int32 [4, 4, 2, 8], P('gx', 'gy', 'gz'), may hold values from 0 to 511
- trainers: int32 [4, 4, 2, 8, 1], P('gx', 'gy', 'gz'), may hold values from 0 to 3; in each aligned block of 8 rows (0 to 7, 8 to 15, ..., all dimensions but the last counted through in order) at most 2 rows name the same one
- conv_first: bfloat16 [32, 108], replicated, may hold values from -0.625 to 0.625
- conv_second: bfloat16 [32, 864], replicated, may hold values from -0.21875 to 0.21875
- conv_third: bfloat16 [6, 32], replicated, may hold values from -1 to 1
Outputs:
- advanced: float32 [4, 32, 128, 256], P(None, 'gx', 'gy', 'gz')
- block_losses: float32 [4, 4, 2, 8], P('gx', 'gy', 'gz')
- first_grad: float32 [32, 108], replicated
- second_grad: float32 [32, 864], replicated
- third_grad: float32 [6, 32], replicated
Inputs may be any that keep to these rules, and one draw needn't show every extreme that they name: `trainers`: among the 8 samples of one device no trainer occurs more than 2 times, and on some device one occurs exactly 2 times.
All inputs are finite; a program needn't handle non-finite values.
Results may differ from a plain program's by a relative error of at most 0.0036.
The roundings to bfloat16 on the way count: a program that leaves them out, or rounds other values in their place, can miss the bound.
Values may be sent and summed in bfloat16 or wider, within the bound.
No kernel may reach another device: no remote copies, remote signals or barrier semaphores. Data moves between devices by JAX's collectives and lax.ppermute only.
A program may use at most 128 MiB of HBM per device.

v0:
```python
import functools

import jax
import jax.numpy as jnp
from jax import lax
from jax.experimental import pallas as pl
from jax.experimental.pallas import tpu as pltpu
from jax.sharding import PartitionSpec as P

BLK = 4
CAP = 2
SAMP = 8
Z_TILES = 2
NF = 4
VOL = BLK**3
TAPS = [(x, y, z) for x in (-1, 0, 1) for y in (-1, 0, 1) for z in (-1, 0, 1)]
LANES = 128
ROWS = 8
NOUT = 6
CH = 32

time_step = 0.25
buoyancy = 0.5

VMEM = pl.BlockSpec(memory_space=pltpu.VMEM)
SMEM = pl.BlockSpec(memory_space=pltpu.SMEM)
HBM = pl.BlockSpec(memory_space=pltpu.HBM)
ANY = pl.BlockSpec(memory_space=pl.ANY)
PARAMS = pltpu.CompilerParams(vmem_limit_bytes=24 * 1024 * 1024)
PACK = pltpu.CompilerParams(vmem_limit_bytes=54944 * 1024)
FULL = (((1,), (1,)), ((), ()))


def iota(shape, axis):
    return lax.broadcasted_iota(jnp.int32, shape, axis)


def odd(axis):
    return lax.axis_index(axis) % 2 == 1


def facing(axis, swap, first, last):
    return jnp.where(odd(axis), first, last) if swap == "a" else jnp.where(odd(axis), last, first)


def prev_next(axis, from_a, from_b):
    return jnp.where(odd(axis), from_a, from_b), jnp.where(odd(axis), from_b, from_a)


class Parts:
    def __init__(self, *parts):
        self.parts, self.tiles = parts, parts[0].shape[0]

    def at_tile(self, index):
        tile, rest = (index[0], index[1:]) if isinstance(index, tuple) else (index, ())
        return self.parts[tile // self.tiles], (tile % self.tiles,) + rest

    def __getitem__(self, index):
        part, place = self.at_tile(index)
        return part[place]

    def __setitem__(self, index, value):
        part, place = self.at_tile(index)
        part[place] = value


class Sides:
    def __init__(self, chunks, x_b, x_a, z_both, y_b=None, y_a=None):
        self.chunks = chunks
        self.x_a, self.x_b, self.y_a, self.y_b, self.z_both = x_a, x_b, y_a, y_b, z_both

    def along_x(self, f, c):
        tile = f * self.chunks + c
        return prev_next("gx", self.x_a[tile], self.x_b[tile])

    def along_y(self, f, depth=0):
        tile = depth * (NF + 1) + f
        return prev_next("gy", self.y_a[tile], self.y_b[tile])


def pair_of(f, c, planes, chunks):
    span = 2 * planes * chunks
    return f * span // LANES, f * span % LANES + 2 * planes * c


def add_pair(packed, tile, lane):
    moved = pltpu.roll(tile, lane + 1, 1)
    at = iota(tile.shape, 1)
    return jnp.where((at == lane) | (at == lane + 1), moved, packed)


def cut_x(f, array, x_b, x_a):
    planes, rows, _ = array.shape
    chunks = rows // ROWS
    for c in range(chunks):
        part = slice(ROWS * c, ROWS * c + ROWS)
        ends = array[0, part], array[planes - 1, part]
        x_b[f * chunks + c] = facing("gx", "b", *ends)
        x_a[f * chunks + c] = facing("gx", "a", *ends)


def pack_faces(fields_far, visc_far, x_b, x_a, z_both, y_b, y_a, fields, visc, sems):
    _, planes, rows, _ = fields.shape
    chunks = rows // ROWS
    copies = [
        pltpu.make_async_copy(fields_far, fields, sems.at[0]),
        pltpu.make_async_copy(visc_far, visc, sems.at[1]),
    ]
    for copy in copies:
        copy.start()
    arrays = [fields.at[f] for f in range(NF)] + [visc]
    packed = [jnp.zeros((ROWS, LANES), jnp.float32) for _ in range(z_both.shape[0])]
    for f, array in enumerate(arrays):
        if f == 0 or f == NF:
            copies[f // NF].wait()
        cut_x(f, array, x_b, x_a)
        for depth in range(2):
            ends = array[:, depth, :], array[:, rows - 1 - depth, :]
            y_b[depth * (NF + 1) + f] = facing("gy", "b", *ends)
            y_a[depth * (NF + 1) + f] = facing("gy", "a", *ends)
        for c in range(chunks):
            tile, lane = pair_of(f, c, planes, chunks)
            for x in range(planes):
                cells = array[x, ROWS * c : ROWS * c + ROWS]
                packed[tile] = add_pair(packed[tile], cells, lane + 2 * x)
    for tile, value in enumerate(packed):
        z_both[tile] = value


def flux(lower, upper, dimension):
    speed = 0.25 * (lower[dimension] + upper[dimension])
    mean_visc = 0.5 * (lower[NF] + upper[NF])
    return [speed * (a + b) - mean_visc * (b - a) for a, b in zip(lower[:NF], upper[:NF])]


def interior(fields, visc, partial):
    _, planes, rows, _ = fields.shape
    chunks = rows // ROWS
    end_row = iota((ROWS, LANES), 0) == ROWS - 1
    end_lane = iota((ROWS, LANES), 1) == LANES - 1
    every = range(NF + 1)

    def cell(f, x, part):
        return fields[f, x, part, :] if f < NF else visc[x, part, :]

    def plane(x, lowers):
        uppers = []
        last = x == planes - 1
        beyond = jnp.minimum(x + 1, planes - 1)
        behind = [jnp.zeros((ROWS, LANES), jnp.float32)] * NF
        for c in range(chunks):
            part = slice(ROWS * c, ROWS * c + ROWS)
            here = [cell(f, x, part) for f in every]
            after = [cell(f, beyond, part) for f in every]
            upper = flux(here, after, 0)
            upper = [jnp.where(last, 0.0, u) for u in upper]
            total = [b - a for a, b in zip(lowers[c], upper)]
            uppers.append(upper)
            above = [pltpu.roll(h, ROWS - 1, 0) for h in here]
            if c + 1 < chunks:
                first = slice(ROWS * c + ROWS, ROWS * c + ROWS + 1)
                above = [jnp.where(end_row, cell(f, x, first), above[f]) for f in every]
            upper = flux(here, above, 1)
            lower = [pltpu.roll(jnp.where(end_row, b, u), 1, 0) for b, u in zip(behind, upper)]
            if c + 1 == chunks:
                upper = [jnp.where(end_row, 0.0, u) for u in upper]
            behind = upper
            total = [t + (b - a) for t, a, b in zip(total, lower, upper)]
            right = [pltpu.roll(h, LANES - 1, 1) for h in here]
            upper = [jnp.where(end_lane, 0.0, u) for u in flux(here, right, 2)]
            lower = [pltpu.roll(u, 1, 1) for u in upper]
            total = [t + (b - a) for t, a, b in zip(total, lower, upper)]
            updated = [q - time_step * t for q, t in zip(here[:NF], total)]
            updated[2] = updated[2] + (time_step * buoyancy) * here[3]
            for f in range(NF):
                partial[f, x, part, :] = updated[f]
        return uppers

    zeros = [[jnp.zeros((ROWS, LANES), jnp.float32)] * NF for _ in range(chunks)]
    lax.fori_loop(0, planes, plane, zeros)


def rims_without_ends(fields, visc, sides, rims):
    rows = fields.shape[2]
    every = range(NF + 1)
    end_row = iota((ROWS, LANES), 0) == ROWS - 1
    end_lane = iota((ROWS, LANES), 1) == LANES - 1

    def own(row):
        return [fields[f, :, row, :] for f in range(NF)] + [visc[:, row, :]]

    for side in range(2):
        here = [sides.along_y(f)[side] for f in every]
        beyond = [sides.along_y(f, 1)[side] for f in every]
        below, above = (beyond, own(0)) if side == 0 else (own(rows - 1), beyond)
        total = [b - a for a, b in zip(flux(below, here, 1), flux(here, above, 1))]
        for dimension, axis, end in ((0, 0, end_row), (2, 1, end_lane)):
            after = [pltpu.roll(h, h.shape[axis] - 1, axis) for h in here]
            upper = [jnp.where(end, 0.0, u) for u in flux(here, after, dimension)]
            total = [t + (u - pltpu.roll(u, 1, axis)) for t, u in zip(total, upper)]
        updated = [q - time_step * t for q, t in zip(here[:NF], total)]
        updated[2] = updated[2] + (time_step * buoyancy) * here[3]
        for f in range(NF):
            rims[side * NF + f] = updated[f]


def rims_with_ends(rims, sides, later):
    row = iota((ROWS, LANES), 0)
    lane = iota((ROWS, LANES), 1)
    every = range(NF + 1)
    whole = []
    for side in range(2):
        here = [sides.along_y(f)[side] for f in every]
        tile = NF * later.chunks + side
        before, after = prev_next("gx", later.x_a[tile], later.x_b[tile])
        low = flux([before[f : f + 1] for f in every], [h[:1] for h in here], 0)
        high = flux([h[ROWS - 1 :] for h in here], [after[f : f + 1] for f in every], 0)
        columns = later.z_both[Z_TILES]
        left, right = [], []
        for f in every:
            both = pltpu.roll(columns, LANES - 1 - 2 * (side * (NF + 1) + f), 1)
            left.append(pltpu.roll(jnp.where(lane == LANES - 1, both, here[f]), 1, 1))
            right.append(pltpu.roll(jnp.where(lane == 0, both, here[f]), LANES - 1, 1))
        lower, upper = flux(left, here, 2), flux(here, right, 2)
        ends = []
        for f in range(NF):
            value = rims[side * NF + f]
            value = value + time_step * jnp.where(row == 0, low[f], 0.0)
            value = value - time_step * jnp.where(row == ROWS - 1, high[f], 0.0)
            value = value + time_step * jnp.where(lane == 0, lower[f], 0.0)
            ends.append(value - time_step * jnp.where(lane == LANES - 1, upper[f], 0.0))
        whole.append(ends)
    return whole


def interior_first(samples_far, trainers_far, fields, visc, conv_first, conv_third, partial, w_first,
                   w_third, w_third_t, drawn, samples, trainers, sems):
    copies = [
        pltpu.make_async_copy(samples_far, samples, sems.at[0]),
        pltpu.make_async_copy(trainers_far, trainers, sems.at[1]),
    ]
    for copy in copies:
        copy.start()
    interior(fields, visc, partial)
    ahead = conv_first.shape[1]
    w_first[:, :ahead] = conv_first[...]
    w_first[:, ahead:] = jnp.zeros((CH, w_first.shape[1] - ahead), jnp.bfloat16)
    third = conv_third[...].astype(jnp.float32)
    third = jnp.concatenate([third, jnp.zeros((w_third.shape[0] - NOUT, CH), jnp.float32)], 0)
    w_third[...] = third.astype(jnp.bfloat16)
    w_third_t[...] = third.T.astype(jnp.bfloat16)
    for copy in copies:
        copy.wait()
    at, row = iota((ROWS, LANES), 1), iota((ROWS, LANES), 0)
    table = jnp.zeros((ROWS, LANES), jnp.int32)
    for j in range(samples.shape[0]):
        table = jnp.where(at == j, jnp.where(row == 0, samples[j], trainers[j]), table)
    drawn[...] = table


def interior_second(middle, visc, fields, y_b, y_a, conv_second, partial, rims, w_second_t):
    interior(middle, visc, partial)
    rims_without_ends(fields, visc, Sides(0, None, None, None, y_b, y_a), rims)
    w_second_t[...] = conv_second[...].astype(jnp.float32).T.astype(jnp.bfloat16)


def z_terms(own, other, visc_own, visc_other):
    lane = iota((ROWS, LANES), 1)
    second = lane % 2 == 1
    span = LANES // 2

    def ends(mine, theirs):
        lower = jnp.where(second, pltpu.roll(theirs, 1, 1), mine)
        return lower, jnp.where(second, mine, pltpu.roll(theirs, LANES - 1, 1))

    def twice(tile):
        return jnp.where(lane < span, tile, pltpu.roll(tile, span, 1))

    pairs = [ends(a, b) for a, b in zip(own, other)]
    speed = [twice(end) for end in pairs[2 * span // LANES]]
    visc = [twice(end) for end in ends(visc_own, visc_other)]
    speed = 0.25 * (speed[0] + speed[1])
    mean_visc = 0.5 * (visc[0] + visc[1])
    through = [speed * (a + b) - mean_visc * (b - a) for a, b in pairs]
    return [jnp.where(second, time_step, -time_step) * t for t in through]


def close(fields, visc, partial, halo, visc_halo, y_faces, z_own, visc_z_own, y_terms, emit):
    _, planes, rows, _ = fields.shape
    chunks = rows // ROWS
    every = range(NF + 1)
    row = iota((ROWS, LANES), 0)
    lane_at = iota((ROWS, LANES), 1)
    ends = (lane_at == 0) | (lane_at == LANES - 1)

    def cell(f, *index):
        return fields[(f,) + index] if f < NF else visc[index]

    def sides(f):
        return halo if f < NF else visc_halo

    lower = flux(y_faces[0], [cell(f, slice(None), 0) for f in every], 1)
    upper = flux([cell(f, slice(None), rows - 1) for f in every], y_faces[1], 1)
    for f in range(NF):
        y_terms[0, f] = time_step * lower[f]
        y_terms[1, f] = -time_step * upper[f]
    tiles = 2 * NF * planes * chunks // LANES
    terms = z_terms([z_own[t] for t in range(tiles)], [halo.z_both[t] for t in range(tiles)],
                    visc_z_own[tiles], visc_halo.z_both[tiles])
    for c in range(chunks):
        part = slice(ROWS * c, ROWS * c + ROWS)
        before, after = zip(*[sides(f).along_x(f, c) for f in every])
        low = flux(before, [cell(f, 0, part) for f in every], 0)
        high = flux([cell(f, planes - 1, part) for f in every], after, 0)
        for x in range(planes):
            for f in range(NF):
                tile, lane = pair_of(f, c, planes, chunks)
                moved = pltpu.roll(terms[tile], LANES - 1 - lane - 2 * x, 1)
                value = partial[f, x, part, :] + jnp.where(ends, moved, 0.0)
                if x == 0:
                    value = value + time_step * low[f]
                if x == planes - 1:
                    value = value - time_step * high[f]
                if c == 0:
                    value = value + jnp.where(row == 0, y_terms[0, f, x : x + 1, :], 0.0)
                if c == chunks - 1:
                    value = value + jnp.where(row == ROWS - 1, y_terms[1, f, x : x + 1, :], 0.0)
                emit(f, x, c, value)


def close_first(fields, visc, partial, z_own, x_from_b, x_from_a, z_other, y_from_b, y_from_a,
                middle, x_b, x_a_low, x_a_high, z_both, y_terms):
    x_a = Parts(x_a_low, x_a_high)
    _, planes, rows, _ = fields.shape
    chunks = rows // ROWS
    halo = Sides(chunks, x_from_b, x_from_a, z_other, y_from_b, y_from_a)
    packed = [jnp.zeros((ROWS, LANES), jnp.float32) for _ in range(Z_TILES + 1)]
    y_faces = list(zip(*[halo.along_y(f) for f in range(NF + 1)]))

    def emit(f, x, c, tile):
        middle[f, x, ROWS * c : ROWS * c + ROWS, :] = tile
        at, lane = pair_of(f, c, planes, chunks)
        packed[at] = add_pair(packed[at], tile, lane + 2 * x)

    for side in range(2):
        for f in range(NF + 1):
            face = y_faces[side][f]
            packed[-1] = add_pair(packed[-1], face, 2 * (side * (NF + 1) + f))
            x_b[NF * chunks + side, f : f + 1, :] = facing("gx", "b", face[:1], face[planes - 1 :])
            x_a[NF * chunks + side, f : f + 1, :] = facing("gx", "a", face[:1], face[planes - 1 :])
    close(fields, visc, partial, halo, halo, y_faces, z_own, z_own, y_terms, emit)
    for at in range(z_both.shape[0]):
        z_both[at] = packed[at] if at <= Z_TILES else jnp.zeros((ROWS, LANES), jnp.float32)
    for f in range(NF):
        cut_x(f, middle.at[f], x_b, x_a)


def inside_masks():
    at = iota((1, LANES), 1) % VOL
    coords = (at // (BLK * BLK), at // BLK % BLK, at % BLK)
    along = []
    for coord in coords:
        along.append({
            -1: jnp.where(coord > 0, 1.0, 0.0),
            0: jnp.ones((1, LANES), jnp.float32),
            1: jnp.where(coord < BLK - 1, 1.0, 0.0),
        })
    return along


def move_of(tap):
    return tap[0] * BLK * BLK + tap[1] * BLK + tap[2]


def shifted(tile, tap, along):
    move = move_of(tap)
    if move == 0:
        return tile
    mask = along[0][tap[0]] * along[1][tap[1]] * along[2][tap[2]]
    return pltpu.roll(tile, (-move) % LANES, 1) * mask


def box(tile, along):
    for dimension, step in enumerate((BLK * BLK, BLK, 1)):
        ahead = pltpu.roll(tile, LANES - step, 1) * along[dimension][1]
        behind = pltpu.roll(tile, step, 1) * along[dimension][-1]
        tile = (behind + tile) + ahead
    return tile / 27.0


def sigmoid(values):
    return 1.0 / (1.0 + jnp.exp(-values))


PICKED = (0, 1, 2, 3, 0, 1, 2, 3, 0, 1, 2, 0, 0, 1, -1, -1, 0, 1, 2, 1, 2, 2, -1, -1)


def pick_rows():
    out, field = iota((32, NF * ROWS), 0), iota((32, NF * ROWS), 1) // ROWS
    table = jnp.zeros((32, NF * ROWS), jnp.float32)
    for i, f in enumerate(PICKED):
        table = jnp.where((out == i) & (field == f), 1.0, table)
    return table.astype(jnp.bfloat16)


def pick_blocks(advanced, samples, count):
    _, _, rows, lanes = advanced.shape
    along_y, along_z = rows // BLK, lanes // BLK
    row = iota((ROWS, LANES), 0)
    lane_at = iota((ROWS, LANES), 1)
    pick = pick_rows()
    out = []
    for j in range(0, count, 2):
        parts = [jnp.zeros((ROWS, LANES), jnp.float32) for _ in range(NF)]
        uppers = []
        for half in range(2):
            block = samples[j + half]
            block_x = block // (along_y * along_z)
            block_y = block // along_z % along_y
            block_z = block % along_z
            uppers.append(block_y % 2)
            start = pl.multiple_of(block_y // 2 * ROWS, ROWS)
            for x in range(BLK):
                turn = lax.rem(VOL * half + BLK * BLK * x - BLK * block_z + LANES, LANES)
                wanted = lane_at // BLK == (VOL * half + BLK * BLK * x) // BLK
                for f in range(NF):
                    tile = advanced[f, block_x * BLK + x, pl.ds(start, ROWS), :]
                    parts[f] = jnp.where(wanted, pltpu.roll(tile, turn, 1), parts[f])
        upper = jnp.where(lane_at < VOL, uppers[0], uppers[1])
        valid = row // BLK == upper
        for f in range(NF):
            for bit in (1, 2):
                moved = pltpu.roll(parts[f], BLK * bit, 1)
                parts[f] = jnp.where(row // bit % 2 == 1, moved, parts[f])
            parts[f] = jnp.where(valid, parts[f], 0.0)
        stacked = jnp.concatenate(parts, 0).astype(jnp.bfloat16)
        out.append(jnp.dot(pick, stacked, preferred_element_type=jnp.float32))
    return out


def closure(advanced, samples, trainers, loads, w_first, w_second, w_second_t, w_third,
            w_third_t, devices_all, stack_first, stack_mid, rows_out, send, slots, inline, place, leaving):
    count = len(samples)
    pairs = count // 2
    cols = [slice(LANES * m, LANES * m + LANES) for m in range(pairs)]
    along = inside_masks()
    lane_at = iota((ROWS, LANES), 1)
    row = iota((ROWS, LANES), 0)

    pos_x, pos_y, pos_z, count_y, count_z = place
    picked = pick_blocks(advanced, samples, count)
    values = [p[:ROWS] for p in picked]
    targets = []
    for p in picked:
        first, second = p[ROWS : 2 * ROWS], p[2 * ROWS : 3 * ROWS]
        targets.append(box(first * second, along) - box(first, along) * box(second, along))

    for m, tile in enumerate(values):
        for t in range(0, 28, 2):
            piece = shifted(tile, TAPS[t], along)
            later = shifted(tile, TAPS[t + 1], along) if t + 1 < 27 else jnp.zeros_like(tile)
            stack_first[BLK * t : BLK * t + ROWS, cols[m]] = jnp.where(row < NF, piece, later)
    stack_in = stack_first[...].astype(jnp.bfloat16)
    pre_first = jnp.dot(w_first, stack_in, preferred_element_type=jnp.float32)
    gate_first = sigmoid(pre_first)
    hidden_first = (pre_first * gate_first).astype(jnp.bfloat16).astype(jnp.float32)
    for m in range(pairs):
        tile = hidden_first[:, cols[m]]
        for k, tap in enumerate(TAPS):
            stack_mid[CH * k : CH * k + CH, cols[m]] = shifted(tile, tap, along).astype(jnp.bfloat16)
    leaving.start()
    pre_second = jnp.dot(w_second, stack_mid[...], preferred_element_type=jnp.float32)
    gate_second = sigmoid(pre_second)
    hidden_second = (pre_second * gate_second).astype(jnp.bfloat16)
    predicted = jnp.dot(w_third, hidden_second, preferred_element_type=jnp.float32)

    misfit = predicted[:ROWS] - jnp.concatenate(targets, 1)
    square = jnp.sum(misfit * misfit, axis=0, keepdims=True)
    sample_at = iota((ROWS, count * VOL), 1) // VOL
    mine = sample_at == iota((ROWS, count * VOL), 0)
    losses = jnp.sum(jnp.where(mine, square, 0.0), axis=1, keepdims=True) / (NOUT * VOL)
    if loads is None:
        load = jnp.full((ROWS, 1), float(count_y * CAP), jnp.float32)
    else:
        owner = jnp.zeros((ROWS, LANES), jnp.int32)
        for j in range(count):
            owner = jnp.where(row == j, trainers[j], owner)
        load = jnp.sum(jnp.where(lane_at == owner, loads, 0.0), axis=1, keepdims=True)
    share = 1.0 / (devices_all * jnp.maximum(load, 1.0))
    scale = share * (2.0 / (NOUT * VOL))
    scale_at = jnp.sum(jnp.where(mine, scale, 0.0), axis=0, keepdims=True)
    grad_pred = (misfit * scale_at).astype(jnp.bfloat16)
    grad_pred = jnp.concatenate([grad_pred, jnp.zeros_like(grad_pred)], 0)

    upper = jnp.dot(w_third_t, grad_pred, preferred_element_type=jnp.float32)
    slope = gate_second * (1.0 + pre_second * (1.0 - gate_second))
    grad_mid = (upper * slope).astype(jnp.bfloat16)
    grad_second = lax.dot_general(grad_mid, stack_mid[...], FULL, preferred_element_type=jnp.float32)
    third = jnp.concatenate([grad_pred, jnp.zeros((LANES - 16, count * VOL), jnp.bfloat16)], 0)
    grad_third = lax.dot_general(hidden_second, third, FULL, preferred_element_type=jnp.float32)

    spread = jnp.dot(w_second_t, grad_mid, preferred_element_type=jnp.float32)
    lower = []
    for m in range(pairs):
        terms = [
            shifted(spread[CH * k : CH * k + CH, cols[m]], tuple(-o for o in tap), along)
            for k, tap in enumerate(TAPS)
        ]
        lower.append(functools.reduce(jnp.add, terms))
    lower = jnp.concatenate(lower, 1)
    slope = gate_first * (1.0 + pre_first * (1.0 - gate_first))
    grad_entry = (lower * slope).astype(jnp.bfloat16)
    grad_first = lax.dot_general(grad_entry, stack_in, FULL, preferred_element_type=jnp.float32)

    whole = CH * 27 // LANES
    rest = CH * 27 - whole * LANES
    for t in range(whole):
        rows_out[:, t, :] = grad_second[:, LANES * t : LANES * t + LANES]
    mixed = jnp.concatenate([grad_second[:, whole * LANES :], jnp.zeros((CH, LANES - rest), jnp.float32)], 1)
    mixed = mixed + pltpu.roll(grad_third, rest, 1)
    tail = LANES - grad_first.shape[1]
    rows_out[:, whole + 1, :] = jnp.concatenate([grad_first, jnp.zeros((CH, tail), jnp.float32)], 1)

    offset = rest + ROWS if inline else 0
    height = CH if inline else slots.shape[0]
    slot_rows = iota((height, LANES), 0)
    slot_lanes = iota((height, LANES), 1)
    placed = jnp.zeros((height, LANES), jnp.float32)
    for j in range(count):
        name = trainers[j]
        rank = jnp.int32(0)
        for i in range(j):
            rank = rank + jnp.where(trainers[i] == name, 1, 0)
        target = (pos_x * count_y + name) * count_z + pos_z
        slot = offset + pos_y * CAP + rank
        hit = (slot_rows == target) & (slot_lanes == slot)
        placed = jnp.where(hit, losses[j : j + 1, :], placed)
    high = placed.astype(jnp.bfloat16).astype(jnp.float32)
    placed = high + pltpu.roll(placed - high, count_y * CAP, 1)
    if inline:
        mixed = mixed + placed
    else:
        slots[:, 0, :] = placed.astype(jnp.bfloat16)
    rows_out[:, whole, :] = mixed
    send[...] = rows_out[...].astype(jnp.bfloat16)


def second_step(sizes, inline, drawn, middle, visc, partial, rims, vz_own, vx_b, vx_a, vz_other, vy_b, vy_a,
                z_own, x_b, z_other, x_a_low, x_a_high, *rest):
    loads, rest = (None, rest) if sizes["gy"] * CAP == SAMP else (rest[0][...], rest[1:])
    w_first, w_second, w_second_t, w_third, w_third_t, advanced_far, send = rest[:7]
    slots = None if inline else rest[7]
    stack_first, stack_mid, rows_out, y_terms, advanced, sem = rest[-6:]
    chunks = middle.shape[2] // ROWS
    halo = Sides(chunks, x_b, Parts(x_a_low, x_a_high), z_other)
    visc_halo = Sides(chunks, vx_b, vx_a, vz_other, vy_b, vy_a)
    y_faces = rims_with_ends(rims, visc_halo, halo)
    y_faces = [face + [visc_halo.along_y(NF)[side]] for side, face in enumerate(y_faces)]
    count = stack_mid.shape[1] // VOL
    samples = [drawn[0, j] for j in range(count)]
    trainers = [drawn[1, j] for j in range(count)]

    def emit(f, x, c, tile):
        advanced[f, x, ROWS * c : ROWS * c + ROWS, :] = tile

    close(middle, visc, partial, halo, visc_halo, y_faces, z_own, vz_own, y_terms, emit)
    leaving = pltpu.make_async_copy(advanced, advanced_far, sem)
    place = (lax.axis_index("gx"), lax.axis_index("gy"), lax.axis_index("gz"), sizes["gy"], sizes["gz"])
    closure(advanced, samples, trainers, loads, w_first[...], w_second[...],
            w_second_t[...], w_third[...], w_third_t[...],
            float(sizes["gx"] * sizes["gy"] * sizes["gz"]), stack_first, stack_mid, rows_out,
            send, slots, inline, place, leaving)
    leaving.wait()


def add_up(arrived, spread, own):
    total = jnp.sum(arrived[...].astype(jnp.float32), axis=0)
    own[...] = total
    rounded = total.astype(jnp.bfloat16)
    for i in range(spread.shape[0]):
        spread[i] = rounded


def unpack(where, gathered, own, first, second, third, losses, wide):
    row, lane = where
    count = losses.shape[3]
    high = own[row : row + 1, lane : lane + count]
    losses[0, 0] = high + own[row : row + 1, lane + count : lane + 2 * count]
    wide[...] = gathered[...].astype(jnp.float32)
    whole = second.shape[1] // LANES
    rest = second.shape[1] - whole * LANES
    for t in range(whole):
        second[:, LANES * t : LANES * t + LANES] = wide[:, t, :]
    mixed = wide[:, whole, :]
    second[:, LANES * whole :] = mixed[:, :rest]
    third[...] = mixed[:, rest : rest + ROWS].T[:NOUT]
    first[...] = wide[:, whole + 1, :][:, : first.shape[1]]


def shape_of(*dims, dtype=jnp.float32):
    return jax.ShapeDtypeStruct(dims, dtype)


def swap_a(face, axis, sizes):
    return lax.ppermute(face, axis, [(i, i ^ 1) for i in range(sizes[axis])])


def swap_b(face, axis, sizes):
    count = sizes[axis]
    return lax.ppermute(face, axis, [(i, (i + (1 if i % 2 else -1)) % count) for i in range(count)])


def beside(kernel, cells, more_shapes, index, arrays):
    scratch = [pltpu.SMEM(array.shape, jnp.int32) for array in index]
    if index:
        scratch.append(pltpu.SemaphoreType.DMA((len(index),)))
    return pl.pallas_call(
        kernel,
        out_shape=[shape_of(*arrays[0].shape)] + more_shapes,
        in_specs=[ANY] * len(index) + [VMEM] * len(arrays),
        out_specs=[VMEM] * (1 + len(more_shapes)),
        scratch_shapes=scratch,
        compiler_params=PARAMS,
        cost_estimate=pl.CostEstimate(flops=120 * cells, bytes_accessed=36 * cells, transcendentals=0),
        name=kernel.__name__,
    )(*index, *arrays)


def on_device(sizes, fields, visc, samples, trainers, conv_first, conv_second, conv_third):
    _, planes, rows, lanes = fields.shape
    axes = ("gx", "gy", "gz")
    devices_all = sizes["gx"] * sizes["gy"] * sizes["gz"]
    chunks = rows // ROWS
    pairs = planes * chunks
    half = LANES // 2
    samples = samples.reshape(-1)
    trainers = trainers.reshape(-1)

    faces = pl.pallas_call(
        pack_faces,
        out_shape=[
            shape_of((NF + 1) * chunks, ROWS, lanes),
            shape_of((NF + 1) * chunks, ROWS, lanes),
            shape_of(-(-(NF + 1) * pairs // half), ROWS, LANES),
            shape_of(2 * (NF + 1), planes, lanes),
            shape_of(2 * (NF + 1), planes, lanes),
        ],
        in_specs=[HBM, HBM],
        out_specs=[VMEM] * 5,
        scratch_shapes=[
            pltpu.VMEM(fields.shape, jnp.float32),
            pltpu.VMEM(visc.shape, jnp.float32),
            pltpu.SemaphoreType.DMA((2,)),
        ],
        compiler_params=PACK,
        name="pack_faces",
    )(fields, visc)
    x_b, x_a, z_own, y_b, y_a = faces
    halo = [
        swap_b(x_b, "gx", sizes), swap_a(x_a, "gx", sizes), swap_a(z_own, "gz", sizes),
        swap_b(y_b, "gy", sizes), swap_a(y_a, "gy", sizes),
    ]

    own_counts = sizes["gy"] * CAP == SAMP
    counts = []
    if not own_counts:
        named = trainers.reshape(-1, 1) == jnp.arange(LANES, dtype=jnp.int32)[None, :]
        total = lax.psum(jnp.sum(named.astype(jnp.float32), axis=0, keepdims=True), "gy")
        counts = [jnp.broadcast_to(total, (ROWS, LANES))]
    sizes_of = [shape_of(*size, dtype=jnp.bfloat16) for size in ((CH, 28 * NF), (16, CH), (CH, 16))]
    partial, w_first, w_third, w_third_t, drawn = beside(
        interior_first, visc.size, sizes_of + [shape_of(ROWS, LANES, dtype=jnp.int32)],
        (samples, trainers), (fields, visc, conv_first, conv_third),
    )
    y_terms = pltpu.VMEM((2, NF, planes, lanes), jnp.float32)
    middle, x_b, x_a_low, x_a_high, z_later = pl.pallas_call(
        close_first,
        out_shape=[
            shape_of(*fields.shape),
            shape_of(NF * chunks + 2, ROWS, lanes),
            shape_of(NF * chunks // 2 + 1, ROWS, lanes),
            shape_of(NF * chunks // 2 + 1, ROWS, lanes),
            shape_of(NF * chunks // 2 + 2, ROWS, LANES),
        ],
        in_specs=[VMEM] * 9,
        out_specs=[VMEM] * 5,
        scratch_shapes=[y_terms],
        compiler_params=PARAMS,
        name="close_first",
    )(fields, visc, partial, z_own, *halo)
    later = [
        swap_b(x_b, "gx", sizes), swap_a(z_later, "gz", sizes),
        swap_a(x_a_low, "gx", sizes), swap_a(x_a_high, "gx", sizes),
    ]
    partial, rims, w_second_t = beside(
        interior_second, visc.size,
        [shape_of(2 * NF, ROWS, LANES), shape_of(27 * CH, CH, dtype=jnp.bfloat16)],
        (), (middle, visc, fields, *halo[3:], conv_second),
    )

    count = samples.shape[0]
    slot_total = sizes["gy"] * CAP
    tiles = -(-27 * CH // LANES) + 1
    parts = devices_all // CH
    inline = parts == 1 and slot_total <= 12
    out_shape = [shape_of(*fields.shape), shape_of(CH, tiles, LANES, dtype=jnp.bfloat16)]
    if not inline:
        out_shape.append(shape_of(devices_all, 1, LANES, dtype=jnp.bfloat16))
    advanced, send, *slots = pl.pallas_call(
        functools.partial(second_step, sizes, inline),
        out_shape=out_shape,
        in_specs=[VMEM] * (21 + len(counts)),
        out_specs=[ANY] + [VMEM] * (len(out_shape) - 1),
        scratch_shapes=[
            pltpu.VMEM((28 * NF, count * VOL), jnp.float32),
            pltpu.VMEM((27 * CH, count * VOL), jnp.bfloat16),
            pltpu.VMEM((CH, tiles, LANES), jnp.float32),
            y_terms,
            pltpu.VMEM(fields.shape, jnp.float32),
            pltpu.SemaphoreType.DMA,
        ],
        compiler_params=PARAMS,
        name="second_step",
    )(drawn, middle, visc, partial, rims, z_own, *halo, z_later, *later, *counts,
      w_first, conv_second, w_second_t, w_third, w_third_t)

    if not inline:
        send = jnp.concatenate([send.reshape(devices_all, tiles // parts, LANES), slots[0]], 1)
    arrived = lax.all_to_all(send, axes, split_axis=0, concat_axis=0, tiled=True)
    if inline:
        where = (27 * CH // LANES, 27 * CH % LANES + ROWS)
    else:
        where = (send.shape[1] - 1, 0)
    spread, own = pl.pallas_call(
        add_up,
        out_shape=[shape_of(*send.shape, dtype=jnp.bfloat16), shape_of(*send.shape[1:])],
        in_specs=[VMEM],
        out_specs=[VMEM] * 2,
        compiler_params=PARAMS,
        name="add_up",
    )(arrived)
    if not inline:
        spread = spread[:, :-1, :]
    gathered = lax.all_to_all(spread, axes, split_axis=0, concat_axis=0, tiled=True)
    first, second, third, block_losses = pl.pallas_call(
        functools.partial(unpack, where),
        out_shape=[
            shape_of(*conv_first.shape),
            shape_of(*conv_second.shape),
            shape_of(*conv_third.shape),
            shape_of(1, 1, 1, slot_total),
        ],
        in_specs=[VMEM] * 2,
        out_specs=[VMEM] * 4,
        scratch_shapes=[pltpu.VMEM((CH, tiles, LANES), jnp.float32)],
        compiler_params=PARAMS,
        name="unpack",
    )(gathered.reshape(CH, tiles, LANES), own)
    return advanced, block_losses, first, second, third


def solution(mesh):
    sizes = dict(mesh.shape)
    in_specs = (
        P(None, "gx", "gy", "gz"),
        P("gx", "gy", "gz"),
        P("gx", "gy", "gz", None),
        P("gx", "gy", "gz", None, None),
        P(),
        P(),
        P(),
    )
    out_specs = (P(None, "gx", "gy", "gz"), P("gx", "gy", "gz", None), P(), P(), P())
    return jax.shard_map(
        functools.partial(on_device, sizes), mesh=mesh, in_specs=in_specs, out_specs=out_specs,
        check_vma=False,
    )
```

profile of v0, /device:TPU:0, one launch (start us, length us, event | category | flops | bytes accessed | tf_op | source)
XLA Modules:
  0.0 41.2 jit_solution(10616661696016993461)
XLA Ops:
  0.6 0.0 copy-start.1
  0.6 0.0 copy-start
  0.7 1.5 %pack_faces.1 = (f32[20,8,128]{2,1,0:T(8,128)S(1)}, f32[20,8,128]{2,1,0:T(8,128)S(1)}, f32[3,8,128]{2,1,0:T(8,128)S(1)}, f32[10,8,128]{2,1,0:T(8,128)S(1)}, f32[10,8,128]{2,1,0:T(8,128)S(1)}) custom-call(f32[4,8,32,128]{3,2,1,0:T(8,128)} %fields.5, f32[8,32,128]{2,1,0:T(8,128)} %visc.7), custom_call_target="tpu_custom_call" | custom-call | tf_op jit(solution)/shard_map/pack_faces/pallas_call | solution.py:639
  2.1 0.0 copy-start.3
  2.1 2.4 %collective-permute-start = (f32[20,8,128]{2,1,0:T(8,128)S(1)}, f32[20,8,128]{2,1,0:T(8,128)S(1)}, u32[]{:S(2)}, u32[]{:S(2)}) collective-permute-start(f32[20,8,128]{2,1,0:T(8,128)S(1)} %get-tuple-element.34), channel_id=1, source_target_pairs={{0,24},{8,16},{16,8},{24,0},{1,25},{9,17},{17,9},{25,1},{2,26},{10... | collective-permute-start | bytes 245768 | tf_op jit(solution)/shard_map/ppermute | solution.py:610
  4.6 0.7 %collective-permute-start.1 = (f32[20,8,128]{2,1,0:T(8,128)S(1)}, f32[20,8,128]{2,1,0:T(8,128)S(1)}, u32[]{:S(2)}, u32[]{:S(2)}) collective-permute-start(f32[20,8,128]{2,1,0:T(8,128)S(1)} %get-tuple-element.35), channel_id=1, source_target_pairs={{0,8},{8,0},{16,24},{24,16},{1,9},{9,1},{17,25},{25,17},{2,10},{10... | collective-permute-start | bytes 245768 | tf_op jit(solution)/shard_map/ppermute | solution.py:605
  5.2 3.6 %collective-permute-start.3 = (f32[10,8,128]{2,1,0:T(8,128)S(1)}, f32[10,8,128]{2,1,0:T(8,128)S(1)}, u32[]{:S(2)}, u32[]{:S(2)}) collective-permute-start(f32[10,8,128]{2,1,0:T(8,128)S(1)} %get-tuple-element.36), channel_id=1, source_target_pairs={{0,6},{2,4},{4,2},{6,0},{1,7},{3,5},{5,3},{7,1},{8,14},{10,12},{12... | collective-permute-start | bytes 122888 | tf_op jit(solution)/shard_map/ppermute | solution.py:610
  8.9 0.0 collective-permute-start.4
  8.9 0.0 copy-start.4
  8.9 1.5 %collective-permute-start.2 = (f32[3,8,128]{2,1,0:T(8,128)S(1)}, f32[3,8,128]{2,1,0:T(8,128)S(1)}, u32[]{:S(2)}, u32[]{:S(2)}) collective-permute-start(f32[3,8,128]{2,1,0:T(8,128)S(1)} %get-tuple-element.33.z_own.vz_own), channel_id=1, source_target_pairs={{0,1},{1,0},{2,3},{3,2},{4,5},{5,4},{6,7},{7,6},{8,9},{9,8},{10,11... | collective-permute-start | bytes 36872 | tf_op jit(solution)/shard_map/ppermute | solution.py:605
  10.4 0.0 copy-start.5
  10.4 0.0 copy-start.6
  10.4 0.0 copy-done.1
  10.4 0.0 copy-done
  10.4 0.0 copy-done.3
  10.4 0.0 copy-done.4
  10.4 0.6 %copy-done.5 = s32[1,1,1,8]{3,2,1,0:T(1,128)S(1)} copy-done((s32[1,1,1,8]{3,2,1,0:T(1,128)S(1)}, s32[1,1,1,8]{3,2,1,0:T(1,128)}, u32[]{:S(2)}) %copy-start.5) | copy-done | bytes 56
  11.0 0.0 copy-done.6
  11.0 1.5 %interior_first.1 = (f32[4,8,32,128]{3,2,1,0:T(8,128)S(1)}, bf16[32,112]{1,0:T(8,128)(2,1)S(1)}, bf16[16,32]{1,0:T(8,128)(2,1)S(1)}, bf16[32,16]{1,0:T(8,128)(2,1)S(1)}, s32[8,128]{1,0:T(8,128)S(1)}) custom-call(s32[8]{0:T(128)S(1)} %bitcast.2, s32[8]{0:T(128)S(1)} %bitcast.3, f32[4,8,32,128]{3,2,1,0:T(8,128)S(1)} %copy-done, f32[8,32,128]{2,1,0:T(8,128)S(1)} %copy-done.1, ...), custom_call_target="tpu_custom_call" | custom-call | flops 3932160 | bytes 1179648 | tf_op jit(solution)/shard_map/interior_first/pallas_call | solution.py:617
  12.5 0.0 collective-permute-done.2.z_other.vz_other
  12.6 0.0 collective-permute-done.3.y_from_b.y_b.vy_b
  12.6 0.3 collective-permute-done.4.y_from_a.y_a.vy_a
  12.9 0.0 collective-permute-done.x_from_b.vx_b
  12.9 0.0 collective-permute-done.1.x_from_a.vx_a
  12.9 0.0 copy-start.2
  12.9 0.7 %close_first.1 = (f32[4,8,32,128]{3,2,1,0:T(8,128)S(1)}, f32[18,8,128]{2,1,0:T(8,128)S(1)}, f32[9,8,128]{2,1,0:T(8,128)S(1)}, f32[9,8,128]{2,1,0:T(8,128)S(1)}, f32[10,8,128]{2,1,0:T(8,128)S(1)}) custom-call(f32[4,8,32,128]{3,2,1,0:T(8,128)S(1)} %copy-done, f32[8,32,128]{2,1,0:T(8,128)S(1)} %copy-done.1, f32[4,8,32,128]{3,2,1,0:T(8,128)S(1)} %get-tuple-element.32.partial, ...), custom_call_target="tpu_custom_call" | custom-call | tf_op jit(solution)/shard_map/close_first/pallas_call | solution.py:676
  13.5 0.1 collective-permute-start.5
  13.6 1.6 %collective-permute-start.6 = (f32[10,8,128]{2,1,0:T(8,128)S(1)}, f32[10,8,128]{2,1,0:T(8,128)S(1)}, u32[]{:S(2)}, u32[]{:S(2)}) collective-permute-start(f32[10,8,128]{2,1,0:T(8,128)S(1)} %get-tuple-element.41.z_own), channel_id=1, source_target_pairs={{0,1},{1,0},{2,3},{3,2},{4,5},{5,4},{6,7},{7,6},{8,9},{9,8},{10,11... | collective-permute-start | bytes 122888 | tf_op jit(solution)/shard_map/ppermute | solution.py:605
  15.2 0.3 collective-permute-start.7
  15.5 0.2 collective-permute-start.8
  15.7 0.0 copy-done.2
  15.7 1.5 %interior_second.1 = (f32[4,8,32,128]{3,2,1,0:T(8,128)S(1)}, f32[8,8,128]{2,1,0:T(8,128)S(1)}, bf16[864,32]{1,0:T(8,128)(2,1)S(1)}) custom-call(f32[4,8,32,128]{3,2,1,0:T(8,128)S(1)} %get-tuple-element.38.middle, f32[8,32,128]{2,1,0:T(8,128)S(1)} %copy-done.1, f32[4,8,32,128]{3,2,1,0:T(8,128)S(1)} %copy-done, ...), custom_call_target="tpu_custom_call" | custom-call | flops 3932160 | bytes 1179648 | tf_op jit(solution)/shard_map/interior_second/pallas_call | solution.py:617
  17.3 0.0 collective-permute-done.7.x_a_low
  17.3 0.0 collective-permute-done.8.x_a_high
  17.3 0.4 %collective-permute-done.6.z_other = f32[10,8,128]{2,1,0:T(8,128)S(1)} collective-permute-done((f32[10,8,128]{2,1,0:T(8,128)S(1)}, f32[10,8,128]{2,1,0:T(8,128)S(1)}, u32[]{:S(2)}, u32[]{:S(2)}) %collective-permute-start.6) | collective-permute-done | bytes 40992 | tf_op jit(solution)/shard_map/ppermute | solution.py:605
  17.7 0.0 collective-permute-done.5.x_b
  17.7 3.1 %second_step.1 = (f32[4,8,32,128]{3,2,1,0:T(8,128)}, bf16[32,8,128]{2,1,0:T(8,128)(2,1)S(1)}) custom-call(s32[8,128]{1,0:T(8,128)S(1)} %get-tuple-element.31.drawn, f32[4,8,32,128]{3,2,1,0:T(8,128)S(1)} %get-tuple-element.38.middle, f32[8,32,128]{2,1,0:T(8,128)S(1)} %copy-done.1, f32[4,8,32,128]{3,2,1,0:T(8,128)S(1)} %get-tuple-element.39.partial, ...), custom_call_target="tpu_custom_call" | custom-call | tf_op jit(solution)/shard_map/second_step/pallas_call | solution.py:709
  20.9 10.6 %all_to_all.10.arrived = bf16[32,8,128]{2,1,0:T(8,128)(2,1)S(1)} all-to-all(bf16[32,8,128]{2,1,0:T(8,128)(2,1)S(1)} %get-tuple-element.50), channel_id=1, replica_groups=mesh['gx'=4,'gy'=4,'gz'=2] {'gx','gy','gz'}, dimensions={0} | all-to-all | bytes 131072 | tf_op jit(solution)/shard_map/all_to_all | solution.py:729
  31.5 9.0 %all_to_all.11.gathered = bf16[32,8,128]{2,1,0:T(8,128)(2,1)S(1)} all-to-all(bf16[32,8,128]{2,1,0:T(8,128)(2,1)S(1)} %get-tuple-element.51), channel_id=1, replica_groups=mesh['gx'=4,'gy'=4,'gz'=2] {'gx','gy','gz'}, dimensions={0} | all-to-all | bytes 131072 | tf_op jit(solution)/shard_map/all_to_all | solution.py:744
  40.4 0.8 %unpack.1 = (f32[32,108]{1,0:T(8,128)}, f32[32,864]{1,0:T(8,128)}, f32[6,32]{1,0:T(8,128)}, f32[1,1,1,8]{3,2,1,0:T(1,128)}) custom-call(bf16[32,8,128]{2,1,0:T(8,128)(2,1)S(1)} %all_to_all.11.gathered, f32[8,128]{1,0:T(8,128)S(1)} %get-tuple-element.52.own), custom_call_target="tpu_custom_call" | custom-call | tf_op jit(solution)/shard_map/unpack/pallas_call | solution.py:745
  (1 shorter events, 0.0 us)
Async XLA Ops:
  0.6 9.8 %copy-start.1 = (f32[8,32,128]{2,1,0:T(8,128)S(1)}, f32[8,32,128]{2,1,0:T(8,128)}, u32[]{:S(2)}) copy-start(f32[8,32,128]{2,1,0:T(8,128)} %visc.7) | copy-start | bytes 393220
  0.6 9.7 %copy-start = (f32[4,8,32,128]{3,2,1,0:T(8,128)S(1)}, f32[4,8,32,128]{3,2,1,0:T(8,128)}, u32[]{:S(2)}) copy-start(f32[4,8,32,128]{3,2,1,0:T(8,128)} %fields.5) | copy-start | bytes 1572868
  2.1 8.3 %copy-start.3 = (bf16[32,108]{1,0:T(8,128)(2,1)S(1)}, bf16[32,108]{1,0:T(8,128)(2,1)}, u32[]{:S(2)}) copy-start(bf16[32,108]{1,0:T(8,128)(2,1)} %conv_first.1) | copy-start | bytes 20740
  2.1 10.7 %collective-permute-start = (f32[20,8,128]{2,1,0:T(8,128)S(1)}, f32[20,8,128]{2,1,0:T(8,128)S(1)}, u32[]{:S(2)}, u32[]{:S(2)}) collective-permute-start(f32[20,8,128]{2,1,0:T(8,128)S(1)} %get-tuple-element.34), channel_id=1, source_target_pairs={{0,24},{8,16},{16,8},{24,0},{1,25},{9,17},{17,9},{25,1},{2,26},{10... | collective-permute-start | bytes 245768 | tf_op jit(solution)/shard_map/ppermute | solution.py:610
  4.6 8.3 %collective-permute-start.1 = (f32[20,8,128]{2,1,0:T(8,128)S(1)}, f32[20,8,128]{2,1,0:T(8,128)S(1)}, u32[]{:S(2)}, u32[]{:S(2)}) collective-permute-start(f32[20,8,128]{2,1,0:T(8,128)S(1)} %get-tuple-element.35), channel_id=1, source_target_pairs={{0,8},{8,0},{16,24},{24,16},{1,9},{9,1},{17,25},{25,17},{2,10},{10... | collective-permute-start | bytes 245768 | tf_op jit(solution)/shard_map/ppermute | solution.py:605
  5.2 7.3 %collective-permute-start.3 = (f32[10,8,128]{2,1,0:T(8,128)S(1)}, f32[10,8,128]{2,1,0:T(8,128)S(1)}, u32[]{:S(2)}, u32[]{:S(2)}) collective-permute-start(f32[10,8,128]{2,1,0:T(8,128)S(1)} %get-tuple-element.36), channel_id=1, source_target_pairs={{0,6},{2,4},{4,2},{6,0},{1,7},{3,5},{5,3},{7,1},{8,14},{10,12},{12... | collective-permute-start | bytes 122888 | tf_op jit(solution)/shard_map/ppermute | solution.py:610
  8.9 4.0 %collective-permute-start.4 = (f32[10,8,128]{2,1,0:T(8,128)S(1)}, f32[10,8,128]{2,1,0:T(8,128)S(1)}, u32[]{:S(2)}, u32[]{:S(2)}) collective-permute-start(f32[10,8,128]{2,1,0:T(8,128)S(1)} %get-tuple-element.37), channel_id=1, source_target_pairs={{0,2},{2,0},{4,6},{6,4},{1,3},{3,1},{5,7},{7,5},{8,10},{10,8},{12,... | collective-permute-start | bytes 122888 | tf_op jit(solution)/shard_map/ppermute | solution.py:605
  8.9 1.5 %copy-start.4 = (bf16[6,32]{1,0:T(8,128)(2,1)S(1)}, bf16[6,32]{1,0:T(8,128)(2,1)}, u32[]{:S(2)}) copy-start(bf16[6,32]{1,0:T(8,128)(2,1)} %conv_third.1) | copy-start | bytes 1156
  8.9 3.7 %collective-permute-start.2 = (f32[3,8,128]{2,1,0:T(8,128)S(1)}, f32[3,8,128]{2,1,0:T(8,128)S(1)}, u32[]{:S(2)}, u32[]{:S(2)}) collective-permute-start(f32[3,8,128]{2,1,0:T(8,128)S(1)} %get-tuple-element.33.z_own.vz_own), channel_id=1, source_target_pairs={{0,1},{1,0},{2,3},{3,2},{4,5},{5,4},{6,7},{7,6},{8,9},{9,8},{10,11... | collective-permute-start | bytes 36872 | tf_op jit(solution)/shard_map/ppermute | solution.py:605
  10.4 0.7 %copy-start.5 = (s32[1,1,1,8]{3,2,1,0:T(1,128)S(1)}, s32[1,1,1,8]{3,2,1,0:T(1,128)}, u32[]{:S(2)}) copy-start(s32[1,1,1,8]{3,2,1,0:T(1,128)} %param.9) | copy-start | bytes 100
  10.4 0.7 %copy-start.6 = (s32[1,1,1,8,1]{3,4,2,1,0:T(1,128)S(1)}, s32[1,1,1,8,1]{3,4,2,1,0:T(1,128)}, u32[]{:S(2)}) copy-start(s32[1,1,1,8,1]{3,4,2,1,0:T(1,128)} %param.10) | copy-start | bytes 100
  12.9 2.9 %copy-start.2 = (bf16[32,864]{1,0:T(8,128)(2,1)S(1)}, bf16[32,864]{1,0:T(8,128)(2,1)}, u32[]{:S(2)}) copy-start(bf16[32,864]{1,0:T(8,128)(2,1)} %rest_1_.1) | copy-start | bytes 165892
  13.5 4.2 %collective-permute-start.5 = (f32[18,8,128]{2,1,0:T(8,128)S(1)}, f32[18,8,128]{2,1,0:T(8,128)S(1)}, u32[]{:S(2)}, u32[]{:S(2)}) collective-permute-start(f32[18,8,128]{2,1,0:T(8,128)S(1)} %get-tuple-element.42), channel_id=1, source_target_pairs={{0,24},{8,16},{16,8},{24,0},{1,25},{9,17},{17,9},{25,1},{2,26},{10... | collective-permute-start | bytes 221192 | tf_op jit(solution)/shard_map/ppermute | solution.py:610
  13.6 4.1 %collective-permute-start.6 = (f32[10,8,128]{2,1,0:T(8,128)S(1)}, f32[10,8,128]{2,1,0:T(8,128)S(1)}, u32[]{:S(2)}, u32[]{:S(2)}) collective-permute-start(f32[10,8,128]{2,1,0:T(8,128)S(1)} %get-tuple-element.41.z_own), channel_id=1, source_target_pairs={{0,1},{1,0},{2,3},{3,2},{4,5},{5,4},{6,7},{7,6},{8,9},{9,8},{10,11... | collective-permute-start | bytes 122888 | tf_op jit(solution)/shard_map/ppermute | solution.py:605
  15.2 2.1 %collective-permute-start.7 = (f32[9,8,128]{2,1,0:T(8,128)S(1)}, f32[9,8,128]{2,1,0:T(8,128)S(1)}, u32[]{:S(2)}, u32[]{:S(2)}) collective-permute-start(f32[9,8,128]{2,1,0:T(8,128)S(1)} %get-tuple-element.43), channel_id=1, source_target_pairs={{0,8},{8,0},{16,24},{24,16},{1,9},{9,1},{17,25},{25,17},{2,10},{10... | collective-permute-start | bytes 110600 | tf_op jit(solution)/shard_map/ppermute | solution.py:605
  15.5 1.8 %collective-permute-start.8 = (f32[9,8,128]{2,1,0:T(8,128)S(1)}, f32[9,8,128]{2,1,0:T(8,128)S(1)}, u32[]{:S(2)}, u32[]{:S(2)}) collective-permute-start(f32[9,8,128]{2,1,0:T(8,128)S(1)} %get-tuple-element.44), channel_id=1, source_target_pairs={{0,8},{8,0},{16,24},{24,16},{1,9},{9,1},{17,25},{25,17},{2,10},{10... | collective-permute-start | bytes 110600 | tf_op jit(solution)/shard_map/ppermute | solution.py:605
where the time goes:
time: 41.4 us; the launch traced here: 41.2 us
  blocking collectives  19.5 us (47%)
  starting transfers between devices  10.4 us (25%)
  Pallas kernels  9.09 us (22%)
  waiting for transfers between devices  0.79 us (2%)
  between operations  0.75 us (2%)
  local copies, waits for them, and re-layouts  0.66 us (2%)
    all_to_all x1, blocking collectives, on_device(): lax.all_to_all(send, axes, split_axis=0, concat_axis=0, tiled=True)  10.6 us
    all_to_all x1, blocking collectives, on_device(): lax.all_to_all(spread, axes, split_axis=0, concat_axis=0, tiled=True)  8.97 us
    ppermute x3, starting transfers between devices, swap_b(): lax.ppermute(face, axis, [(i, (i + (1 if i % 2 else -1)) % count) for i i...  6.12 us
    ppermute x6, starting transfers between devices, swap_a(): return lax.ppermute(face, axis, [(i, i ^ 1) for i in range(sizes[axis])])  4.29 us
    pallas_call x1, Pallas kernels, on_device(): pl.pallas_call(functools.partial(second_step, sizes, inline), out_shape=o...  3.11 us
    pallas_call x2, Pallas kernels, beside(): pl.pallas_call(kernel, out_shape=[shape_of(*arrays[0].shape)] + more_shap...  3 us
    pallas_call x1, Pallas kernels, on_device(): pl.pallas_call(pack_faces, out_shape=[shape_of((NF + 1) * chunks, ROWS, l...  1.46 us
  transfers between devices with their start and end apart: 9, of which 2 were waited for; matrix products, arithmetic and copies ran while one was open for 0% of the time, Pallas kernels for 7%

commit v1 on v0

--- a/solution.py
+++ b/solution.py
@@ -439,7 +439,7 @@
 
 
 def closure(advanced, samples, trainers, loads, w_first, w_second, w_second_t, w_third,
-            w_third_t, devices_all, stack_first, stack_mid, rows_out, send, slots, inline, place, leaving):
+            w_third_t, devices_all, stack_first, stack_mid, rows_out, send, slots, inline, place):
     count = len(samples)
     pairs = count // 2
     cols = [slice(LANES * m, LANES * m + LANES) for m in range(pairs)]
@@ -468,7 +468,6 @@
         tile = hidden_first[:, cols[m]]
         for k, tap in enumerate(TAPS):
             stack_mid[CH * k : CH * k + CH, cols[m]] = shifted(tile, tap, along).astype(jnp.bfloat16)
-    leaving.start()
     pre_second = jnp.dot(w_second, stack_mid[...], preferred_element_type=jnp.float32)
     gate_second = sigmoid(pre_second)
     hidden_second = (pre_second * gate_second).astype(jnp.bfloat16)
@@ -565,11 +564,12 @@
 
     close(middle, visc, partial, halo, visc_halo, y_faces, z_own, vz_own, y_terms, emit)
     leaving = pltpu.make_async_copy(advanced, advanced_far, sem)
+    leaving.start()
     place = (lax.axis_index("gx"), lax.axis_index("gy"), lax.axis_index("gz"), sizes["gy"], sizes["gz"])
     closure(advanced, samples, trainers, loads, w_first[...], w_second[...],
             w_second_t[...], w_third[...], w_third_t[...],
             float(sizes["gx"] * sizes["gy"] * sizes["gz"]), stack_first, stack_mid, rows_out,
-            send, slots, inline, place, leaving)
+            send, slots, inline, place)
     leaving.wait()
 
 

time: 41.4 us -> 41.4 us (level)
  no operation moved by 1% of the time
where the time goes in v1:
time: 41.4 us; the launch traced here: 41.2 us
  blocking collectives  19.5 us (47%)
  starting transfers between devices  10.4 us (25%)
  Pallas kernels  9.09 us (22%)
  waiting for transfers between devices  0.79 us (2%)
  between operations  0.75 us (2%)
  local copies, waits for them, and re-layouts  0.66 us (2%)
    all_to_all x1, blocking collectives, on_device(): lax.all_to_all(send, axes, split_axis=0, concat_axis=0, tiled=True)  10.6 us
    all_to_all x1, blocking collectives, on_device(): lax.all_to_all(spread, axes, split_axis=0, concat_axis=0, tiled=True)  8.97 us
    ppermute x3, starting transfers between devices, swap_b(): lax.ppermute(face, axis, [(i, (i + (1 if i % 2 else -1)) % count) for i i...  6.12 us
    ppermute x6, starting transfers between devices, swap_a(): return lax.ppermute(face, axis, [(i, i ^ 1) for i in range(sizes[axis])])  4.29 us
    pallas_call x1, Pallas kernels, on_device(): pl.pallas_call(functools.partial(second_step, sizes, inline), out_shape=o...  3.11 us
    pallas_call x2, Pallas kernels, beside(): pl.pallas_call(kernel, out_shape=[shape_of(*arrays[0].shape)] + more_shap...  3 us
    pallas_call x1, Pallas kernels, on_device(): pl.pallas_call(pack_faces, out_shape=[shape_of((NF + 1) * chunks, ROWS, l...  1.46 us
  transfers between devices with their start and end apart: 9, of which 2 were waited for; matrix products, arithmetic and copies ran while one was open for 0% of the time, Pallas kernels for 7%

profile of v1, /device:TPU:0, one launch (start us, length us, event | category | flops | bytes accessed | tf_op | source)
XLA Modules:
  0.0 41.2 jit_solution(10616661696016993461)
XLA Ops:
  0.6 0.0 copy-start.1
  0.6 0.0 copy-start
  0.7 1.5 %pack_faces.1 = (f32[20,8,128]{2,1,0:T(8,128)S(1)}, f32[20,8,128]{2,1,0:T(8,128)S(1)}, f32[3,8,128]{2,1,0:T(8,128)S(1)}, f32[10,8,128]{2,1,0:T(8,128)S(1)}, f32[10,8,128]{2,1,0:T(8,128)S(1)}) custom-call(f32[4,8,32,128]{3,2,1,0:T(8,128)} %fields.5, f32[8,32,128]{2,1,0:T(8,128)} %visc.7), custom_call_target="tpu_custom_call" | custom-call | tf_op jit(solution)/shard_map/pack_faces/pallas_call | solution.py:639
  2.1 0.0 copy-start.3
  2.1 2.4 %collective-permute-start = (f32[20,8,128]{2,1,0:T(8,128)S(1)}, f32[20,8,128]{2,1,0:T(8,128)S(1)}, u32[]{:S(2)}, u32[]{:S(2)}) collective-permute-start(f32[20,8,128]{2,1,0:T(8,128)S(1)} %get-tuple-element.34), channel_id=1, source_target_pairs={{0,24},{8,16},{16,8},{24,0},{1,25},{9,17},{17,9},{25,1},{2,26},{10... | collective-permute-start | bytes 245768 | tf_op jit(solution)/shard_map/ppermute | solution.py:610
  4.6 0.7 %collective-permute-start.1 = (f32[20,8,128]{2,1,0:T(8,128)S(1)}, f32[20,8,128]{2,1,0:T(8,128)S(1)}, u32[]{:S(2)}, u32[]{:S(2)}) collective-permute-start(f32[20,8,128]{2,1,0:T(8,128)S(1)} %get-tuple-element.35), channel_id=1, source_target_pairs={{0,8},{8,0},{16,24},{24,16},{1,9},{9,1},{17,25},{25,17},{2,10},{10... | collective-permute-start | bytes 245768 | tf_op jit(solution)/shard_map/ppermute | solution.py:605
  5.2 3.6 %collective-permute-start.3 = (f32[10,8,128]{2,1,0:T(8,128)S(1)}, f32[10,8,128]{2,1,0:T(8,128)S(1)}, u32[]{:S(2)}, u32[]{:S(2)}) collective-permute-start(f32[10,8,128]{2,1,0:T(8,128)S(1)} %get-tuple-element.36), channel_id=1, source_target_pairs={{0,6},{2,4},{4,2},{6,0},{1,7},{3,5},{5,3},{7,1},{8,14},{10,12},{12... | collective-permute-start | bytes 122888 | tf_op jit(solution)/shard_map/ppermute | solution.py:610
  8.9 0.0 collective-permute-start.4
  8.9 0.0 copy-start.4
  8.9 1.5 %collective-permute-start.2 = (f32[3,8,128]{2,1,0:T(8,128)S(1)}, f32[3,8,128]{2,1,0:T(8,128)S(1)}, u32[]{:S(2)}, u32[]{:S(2)}) collective-permute-start(f32[3,8,128]{2,1,0:T(8,128)S(1)} %get-tuple-element.33.z_own.vz_own), channel_id=1, source_target_pairs={{0,1},{1,0},{2,3},{3,2},{4,5},{5,4},{6,7},{7,6},{8,9},{9,8},{10,11... | collective-permute-start | bytes 36872 | tf_op jit(solution)/shard_map/ppermute | solution.py:605
  10.4 0.0 copy-start.5
  10.4 0.0 copy-start.6
  10.4 0.0 copy-done.1
  10.4 0.0 copy-done
  10.4 0.0 copy-done.3
  10.4 0.0 copy-done.4
  10.4 0.6 %copy-done.5 = s32[1,1,1,8]{3,2,1,0:T(1,128)S(1)} copy-done((s32[1,1,1,8]{3,2,1,0:T(1,128)S(1)}, s32[1,1,1,8]{3,2,1,0:T(1,128)}, u32[]{:S(2)}) %copy-start.5) | copy-done | bytes 56
  11.0 0.0 copy-done.6
  11.0 1.5 %interior_first.1 = (f32[4,8,32,128]{3,2,1,0:T(8,128)S(1)}, bf16[32,112]{1,0:T(8,128)(2,1)S(1)}, bf16[16,32]{1,0:T(8,128)(2,1)S(1)}, bf16[32,16]{1,0:T(8,128)(2,1)S(1)}, s32[8,128]{1,0:T(8,128)S(1)}) custom-call(s32[8]{0:T(128)S(1)} %bitcast.2, s32[8]{0:T(128)S(1)} %bitcast.3, f32[4,8,32,128]{3,2,1,0:T(8,128)S(1)} %copy-done, f32[8,32,128]{2,1,0:T(8,128)S(1)} %copy-done.1, ...), custom_call_target="tpu_custom_call" | custom-call | flops 3932160 | bytes 1179648 | tf_op jit(solution)/shard_map/interior_first/pallas_call | solution.py:617
  12.5 0.0 collective-permute-done.2.z_other.vz_other
  12.6 0.0 collective-permute-done.3.y_from_b.y_b.vy_b
  12.6 0.3 collective-permute-done.4.y_from_a.y_a.vy_a
  12.9 0.0 collective-permute-done.x_from_b.vx_b
  12.9 0.0 collective-permute-done.1.x_from_a.vx_a
  12.9 0.0 copy-start.2
  12.9 0.7 %close_first.1 = (f32[4,8,32,128]{3,2,1,0:T(8,128)S(1)}, f32[18,8,128]{2,1,0:T(8,128)S(1)}, f32[9,8,128]{2,1,0:T(8,128)S(1)}, f32[9,8,128]{2,1,0:T(8,128)S(1)}, f32[10,8,128]{2,1,0:T(8,128)S(1)}) custom-call(f32[4,8,32,128]{3,2,1,0:T(8,128)S(1)} %copy-done, f32[8,32,128]{2,1,0:T(8,128)S(1)} %copy-done.1, f32[4,8,32,128]{3,2,1,0:T(8,128)S(1)} %get-tuple-element.32.partial, ...), custom_call_target="tpu_custom_call" | custom-call | tf_op jit(solution)/shard_map/close_first/pallas_call | solution.py:676
  13.5 0.1 collective-permute-start.5
  13.6 1.6 %collective-permute-start.6 = (f32[10,8,128]{2,1,0:T(8,128)S(1)}, f32[10,8,128]{2,1,0:T(8,128)S(1)}, u32[]{:S(2)}, u32[]{:S(2)}) collective-permute-start(f32[10,8,128]{2,1,0:T(8,128)S(1)} %get-tuple-element.41.z_own), channel_id=1, source_target_pairs={{0,1},{1,0},{2,3},{3,2},{4,5},{5,4},{6,7},{7,6},{8,9},{9,8},{10,11... | collective-permute-start | bytes 122888 | tf_op jit(solution)/shard_map/ppermute | solution.py:605
  15.2 0.3 collective-permute-start.7
  15.5 0.2 collective-permute-start.8
  15.7 0.0 copy-done.2
  15.7 1.5 %interior_second.1 = (f32[4,8,32,128]{3,2,1,0:T(8,128)S(1)}, f32[8,8,128]{2,1,0:T(8,128)S(1)}, bf16[864,32]{1,0:T(8,128)(2,1)S(1)}) custom-call(f32[4,8,32,128]{3,2,1,0:T(8,128)S(1)} %get-tuple-element.38.middle, f32[8,32,128]{2,1,0:T(8,128)S(1)} %copy-done.1, f32[4,8,32,128]{3,2,1,0:T(8,128)S(1)} %copy-done, ...), custom_call_target="tpu_custom_call" | custom-call | flops 3932160 | bytes 1179648 | tf_op jit(solution)/shard_map/interior_second/pallas_call | solution.py:617
  17.3 0.0 collective-permute-done.7.x_a_low
  17.3 0.0 collective-permute-done.8.x_a_high
  17.3 0.4 %collective-permute-done.6.z_other = f32[10,8,128]{2,1,0:T(8,128)S(1)} collective-permute-done((f32[10,8,128]{2,1,0:T(8,128)S(1)}, f32[10,8,128]{2,1,0:T(8,128)S(1)}, u32[]{:S(2)}, u32[]{:S(2)}) %collective-permute-start.6) | collective-permute-done | bytes 40992 | tf_op jit(solution)/shard_map/ppermute | solution.py:605
  17.7 0.0 collective-permute-done.5.x_b
  17.7 3.1 %second_step.1 = (f32[4,8,32,128]{3,2,1,0:T(8,128)}, bf16[32,8,128]{2,1,0:T(8,128)(2,1)S(1)}) custom-call(s32[8,128]{1,0:T(8,128)S(1)} %get-tuple-element.31.drawn, f32[4,8,32,128]{3,2,1,0:T(8,128)S(1)} %get-tuple-element.38.middle, f32[8,32,128]{2,1,0:T(8,128)S(1)} %copy-done.1, f32[4,8,32,128]{3,2,1,0:T(8,128)S(1)} %get-tuple-element.39.partial, ...), custom_call_target="tpu_custom_call" | custom-call | tf_op jit(solution)/shard_map/second_step/pallas_call | solution.py:709
  20.9 10.6 %all_to_all.10.arrived = bf16[32,8,128]{2,1,0:T(8,128)(2,1)S(1)} all-to-all(bf16[32,8,128]{2,1,0:T(8,128)(2,1)S(1)} %get-tuple-element.50), channel_id=1, replica_groups=mesh['gx'=4,'gy'=4,'gz'=2] {'gx','gy','gz'}, dimensions={0} | all-to-all | bytes 131072 | tf_op jit(solution)/shard_map/all_to_all | solution.py:729
  31.5 9.0 %all_to_all.11.gathered = bf16[32,8,128]{2,1,0:T(8,128)(2,1)S(1)} all-to-all(bf16[32,8,128]{2,1,0:T(8,128)(2,1)S(1)} %get-tuple-element.51), channel_id=1, replica_groups=mesh['gx'=4,'gy'=4,'gz'=2] {'gx','gy','gz'}, dimensions={0} | all-to-all | bytes 131072 | tf_op jit(solution)/shard_map/all_to_all | solution.py:744
  40.4 0.8 %unpack.1 = (f32[32,108]{1,0:T(8,128)}, f32[32,864]{1,0:T(8,128)}, f32[6,32]{1,0:T(8,128)}, f32[1,1,1,8]{3,2,1,0:T(1,128)}) custom-call(bf16[32,8,128]{2,1,0:T(8,128)(2,1)S(1)} %all_to_all.11.gathered, f32[8,128]{1,0:T(8,128)S(1)} %get-tuple-element.52.own), custom_call_target="tpu_custom_call" | custom-call | tf_op jit(solution)/shard_map/unpack/pallas_call | solution.py:745
  (1 shorter events, 0.0 us)
Async XLA Ops:
  0.6 9.8 %copy-start.1 = (f32[8,32,128]{2,1,0:T(8,128)S(1)}, f32[8,32,128]{2,1,0:T(8,128)}, u32[]{:S(2)}) copy-start(f32[8,32,128]{2,1,0:T(8,128)} %visc.7) | copy-start | bytes 393220
  0.6 9.7 %copy-start = (f32[4,8,32,128]{3,2,1,0:T(8,128)S(1)}, f32[4,8,32,128]{3,2,1,0:T(8,128)}, u32[]{:S(2)}) copy-start(f32[4,8,32,128]{3,2,1,0:T(8,128)} %fields.5) | copy-start | bytes 1572868
  2.1 8.3 %copy-start.3 = (bf16[32,108]{1,0:T(8,128)(2,1)S(1)}, bf16[32,108]{1,0:T(8,128)(2,1)}, u32[]{:S(2)}) copy-start(bf16[32,108]{1,0:T(8,128)(2,1)} %conv_first.1) | copy-start | bytes 20740
  2.1 10.7 %collective-permute-start = (f32[20,8,128]{2,1,0:T(8,128)S(1)}, f32[20,8,128]{2,1,0:T(8,128)S(1)}, u32[]{:S(2)}, u32[]{:S(2)}) collective-permute-start(f32[20,8,128]{2,1,0:T(8,128)S(1)} %get-tuple-element.34), channel_id=1, source_target_pairs={{0,24},{8,16},{16,8},{24,0},{1,25},{9,17},{17,9},{25,1},{2,26},{10... | collective-permute-start | bytes 245768 | tf_op jit(solution)/shard_map/ppermute | solution.py:610
  4.6 8.3 %collective-permute-start.1 = (f32[20,8,128]{2,1,0:T(8,128)S(1)}, f32[20,8,128]{2,1,0:T(8,128)S(1)}, u32[]{:S(2)}, u32[]{:S(2)}) collective-permute-start(f32[20,8,128]{2,1,0:T(8,128)S(1)} %get-tuple-element.35), channel_id=1, source_target_pairs={{0,8},{8,0},{16,24},{24,16},{1,9},{9,1},{17,25},{25,17},{2,10},{10... | collective-permute-start | bytes 245768 | tf_op jit(solution)/shard_map/ppermute | solution.py:605
  5.2 7.3 %collective-permute-start.3 = (f32[10,8,128]{2,1,0:T(8,128)S(1)}, f32[10,8,128]{2,1,0:T(8,128)S(1)}, u32[]{:S(2)}, u32[]{:S(2)}) collective-permute-start(f32[10,8,128]{2,1,0:T(8,128)S(1)} %get-tuple-element.36), channel_id=1, source_target_pairs={{0,6},{2,4},{4,2},{6,0},{1,7},{3,5},{5,3},{7,1},{8,14},{10,12},{12... | collective-permute-start | bytes 122888 | tf_op jit(solution)/shard_map/ppermute | solution.py:610
  8.9 4.0 %collective-permute-start.4 = (f32[10,8,128]{2,1,0:T(8,128)S(1)}, f32[10,8,128]{2,1,0:T(8,128)S(1)}, u32[]{:S(2)}, u32[]{:S(2)}) collective-permute-start(f32[10,8,128]{2,1,0:T(8,128)S(1)} %get-tuple-element.37), channel_id=1, source_target_pairs={{0,2},{2,0},{4,6},{6,4},{1,3},{3,1},{5,7},{7,5},{8,10},{10,8},{12,... | collective-permute-start | bytes 122888 | tf_op jit(solution)/shard_map/ppermute | solution.py:605
  8.9 1.5 %copy-start.4 = (bf16[6,32]{1,0:T(8,128)(2,1)S(1)}, bf16[6,32]{1,0:T(8,128)(2,1)}, u32[]{:S(2)}) copy-start(bf16[6,32]{1,0:T(8,128)(2,1)} %conv_third.1) | copy-start | bytes 1156
  8.9 3.7 %collective-permute-start.2 = (f32[3,8,128]{2,1,0:T(8,128)S(1)}, f32[3,8,128]{2,1,0:T(8,128)S(1)}, u32[]{:S(2)}, u32[]{:S(2)}) collective-permute-start(f32[3,8,128]{2,1,0:T(8,128)S(1)} %get-tuple-element.33.z_own.vz_own), channel_id=1, source_target_pairs={{0,1},{1,0},{2,3},{3,2},{4,5},{5,4},{6,7},{7,6},{8,9},{9,8},{10,11... | collective-permute-start | bytes 36872 | tf_op jit(solution)/shard_map/ppermute | solution.py:605
  10.4 0.7 %copy-start.5 = (s32[1,1,1,8]{3,2,1,0:T(1,128)S(1)}, s32[1,1,1,8]{3,2,1,0:T(1,128)}, u32[]{:S(2)}) copy-start(s32[1,1,1,8]{3,2,1,0:T(1,128)} %param.9) | copy-start | bytes 100
  10.4 0.7 %copy-start.6 = (s32[1,1,1,8,1]{3,4,2,1,0:T(1,128)S(1)}, s32[1,1,1,8,1]{3,4,2,1,0:T(1,128)}, u32[]{:S(2)}) copy-start(s32[1,1,1,8,1]{3,4,2,1,0:T(1,128)} %param.10) | copy-start | bytes 100
  12.9 2.9 %copy-start.2 = (bf16[32,864]{1,0:T(8,128)(2,1)S(1)}, bf16[32,864]{1,0:T(8,128)(2,1)}, u32[]{:S(2)}) copy-start(bf16[32,864]{1,0:T(8,128)(2,1)} %rest_1_.1) | copy-start | bytes 165892
  13.5 4.2 %collective-permute-start.5 = (f32[18,8,128]{2,1,0:T(8,128)S(1)}, f32[18,8,128]{2,1,0:T(8,128)S(1)}, u32[]{:S(2)}, u32[]{:S(2)}) collective-permute-start(f32[18,8,128]{2,1,0:T(8,128)S(1)} %get-tuple-element.42), channel_id=1, source_target_pairs={{0,24},{8,16},{16,8},{24,0},{1,25},{9,17},{17,9},{25,1},{2,26},{10... | collective-permute-start | bytes 221192 | tf_op jit(solution)/shard_map/ppermute | solution.py:610
  13.6 4.1 %collective-permute-start.6 = (f32[10,8,128]{2,1,0:T(8,128)S(1)}, f32[10,8,128]{2,1,0:T(8,128)S(1)}, u32[]{:S(2)}, u32[]{:S(2)}) collective-permute-start(f32[10,8,128]{2,1,0:T(8,128)S(1)} %get-tuple-element.41.z_own), channel_id=1, source_target_pairs={{0,1},{1,0},{2,3},{3,2},{4,5},{5,4},{6,7},{7,6},{8,9},{9,8},{10,11... | collective-permute-start | bytes 122888 | tf_op jit(solution)/shard_map/ppermute | solution.py:605
  15.2 2.1 %collective-permute-start.7 = (f32[9,8,128]{2,1,0:T(8,128)S(1)}, f32[9,8,128]{2,1,0:T(8,128)S(1)}, u32[]{:S(2)}, u32[]{:S(2)}) collective-permute-start(f32[9,8,128]{2,1,0:T(8,128)S(1)} %get-tuple-element.43), channel_id=1, source_target_pairs={{0,8},{8,0},{16,24},{24,16},{1,9},{9,1},{17,25},{25,17},{2,10},{10... | collective-permute-start | bytes 110600 | tf_op jit(solution)/shard_map/ppermute | solution.py:605
  15.5 1.8 %collective-permute-start.8 = (f32[9,8,128]{2,1,0:T(8,128)S(1)}, f32[9,8,128]{2,1,0:T(8,128)S(1)}, u32[]{:S(2)}, u32[]{:S(2)}) collective-permute-start(f32[9,8,128]{2,1,0:T(8,128)S(1)} %get-tuple-element.44), channel_id=1, source_target_pairs={{0,8},{8,0},{16,24},{24,16},{1,9},{9,1},{17,25},{25,17},{2,10},{10... | collective-permute-start | bytes 110600 | tf_op jit(solution)/shard_map/ppermute | solution.py:605

commit v2 on v1

--- a/solution.py
+++ b/solution.py
@@ -547,9 +547,9 @@
 def second_step(sizes, inline, drawn, middle, visc, partial, rims, vz_own, vx_b, vx_a, vz_other, vy_b, vy_a,
                 z_own, x_b, z_other, x_a_low, x_a_high, *rest):
     loads, rest = (None, rest) if sizes["gy"] * CAP == SAMP else (rest[0][...], rest[1:])
-    w_first, w_second, w_second_t, w_third, w_third_t, advanced_far, send = rest[:7]
+    w_first, w_second, w_second_t, w_third, w_third_t, advanced, send = rest[:7]
     slots = None if inline else rest[7]
-    stack_first, stack_mid, rows_out, y_terms, advanced, sem = rest[-6:]
+    stack_first, stack_mid, rows_out, y_terms = rest[-4:]
     chunks = middle.shape[2] // ROWS
     halo = Sides(chunks, x_b, Parts(x_a_low, x_a_high), z_other)
     visc_halo = Sides(chunks, vx_b, vx_a, vz_other, vy_b, vy_a)
@@ -563,14 +563,11 @@
         advanced[f, x, ROWS * c : ROWS * c + ROWS, :] = tile
 
     close(middle, visc, partial, halo, visc_halo, y_faces, z_own, vz_own, y_terms, emit)
-    leaving = pltpu.make_async_copy(advanced, advanced_far, sem)
-    leaving.start()
     place = (lax.axis_index("gx"), lax.axis_index("gy"), lax.axis_index("gz"), sizes["gy"], sizes["gz"])
     closure(advanced, samples, trainers, loads, w_first[...], w_second[...],
             w_second_t[...], w_third[...], w_third_t[...],
             float(sizes["gx"] * sizes["gy"] * sizes["gz"]), stack_first, stack_mid, rows_out,
             send, slots, inline, place)
-    leaving.wait()
 
 
 def add_up(arrived, spread, own):
@@ -581,7 +578,9 @@
         spread[i] = rounded
 
 
-def unpack(where, gathered, own, first, second, third, losses, wide):
+def unpack(where, gathered, own, kept, first, second, third, losses, advanced, wide, sem):
+    leaving = pltpu.make_async_copy(kept, advanced, sem)
+    leaving.start()
     row, lane = where
     count = losses.shape[3]
     high = own[row : row + 1, lane : lane + count]
@@ -595,6 +594,7 @@
     second[:, LANES * whole :] = mixed[:, :rest]
     third[...] = mixed[:, rest : rest + ROWS].T[:NOUT]
     first[...] = wide[:, whole + 1, :][:, : first.shape[1]]
+    leaving.wait()
 
 
 def shape_of(*dims, dtype=jnp.float32):
@@ -706,18 +706,16 @@
     out_shape = [shape_of(*fields.shape), shape_of(CH, tiles, LANES, dtype=jnp.bfloat16)]
     if not inline:
         out_shape.append(shape_of(devices_all, 1, LANES, dtype=jnp.bfloat16))
-    advanced, send, *slots = pl.pallas_call(
+    kept, send, *slots = pl.pallas_call(
         functools.partial(second_step, sizes, inline),
         out_shape=out_shape,
         in_specs=[VMEM] * (21 + len(counts)),
-        out_specs=[ANY] + [VMEM] * (len(out_shape) - 1),
+        out_specs=[VMEM] * len(out_shape),
         scratch_shapes=[
             pltpu.VMEM((28 * NF, count * VOL), jnp.float32),
             pltpu.VMEM((27 * CH, count * VOL), jnp.bfloat16),
             pltpu.VMEM((CH, tiles, LANES), jnp.float32),
             y_terms,
-            pltpu.VMEM(fields.shape, jnp.float32),
-            pltpu.SemaphoreType.DMA,
         ],
         compiler_params=PARAMS,
         name="second_step",
@@ -742,20 +740,21 @@
     if not inline:
         spread = spread[:, :-1, :]
     gathered = lax.all_to_all(spread, axes, split_axis=0, concat_axis=0, tiled=True)
-    first, second, third, block_losses = pl.pallas_call(
+    first, second, third, block_losses, advanced = pl.pallas_call(
         functools.partial(unpack, where),
         out_shape=[
             shape_of(*conv_first.shape),
             shape_of(*conv_second.shape),
             shape_of(*conv_third.shape),
             shape_of(1, 1, 1, slot_total),
+            shape_of(*fields.shape),
         ],
-        in_specs=[VMEM] * 2,
-        out_specs=[VMEM] * 4,
-        scratch_shapes=[pltpu.VMEM((CH, tiles, LANES), jnp.float32)],
+        in_specs=[VMEM, VMEM, ANY],
+        out_specs=[VMEM] * 4 + [ANY],
+        scratch_shapes=[pltpu.VMEM((CH, tiles, LANES), jnp.float32), pltpu.SemaphoreType.DMA],
         compiler_params=PARAMS,
         name="unpack",
-    )(gathered.reshape(CH, tiles, LANES), own)
+    )(gathered.reshape(CH, tiles, LANES), own, kept)
     return advanced, block_losses, first, second, third
 
 

time: 41.4 us -> 41.6 us (level)
    pallas_call x1, Pallas kernels: 0.8 us -> 1.49 us  [on_device(): pl.pallas_call(functools.partial(unpack, where), out_shape=[shape_of(*con...]
    pallas_call x1, Pallas kernels: 3.11 us -> 2.62 us  [on_device(): pl.pallas_call(functools.partial(second_step, sizes, inline), out_shape=o...]
where the time goes in v2:
time: 41.6 us; the launch traced here: 41.5 us
  blocking collectives  19.6 us (47%)
  starting transfers between devices  10.4 us (25%)
  Pallas kernels  9.29 us (22%)
  waiting for transfers between devices  0.79 us (2%)
  between operations  0.74 us (2%)
  local copies, waits for them, and re-layouts  0.66 us (2%)
    all_to_all x1, blocking collectives, on_device(): lax.all_to_all(send, axes, split_axis=0, concat_axis=0, tiled=True)  10.6 us
    all_to_all x1, blocking collectives, on_device(): lax.all_to_all(spread, axes, split_axis=0, concat_axis=0, tiled=True)  8.97 us
    ppermute x3, starting transfers between devices, swap_b(): lax.ppermute(face, axis, [(i, (i + (1 if i % 2 else -1)) % count) for i i...  6.12 us
    ppermute x6, starting transfers between devices, swap_a(): return lax.ppermute(face, axis, [(i, i ^ 1) for i in range(sizes[axis])])  4.29 us
    pallas_call x2, Pallas kernels, beside(): pl.pallas_call(kernel, out_shape=[shape_of(*arrays[0].shape)] + more_shap...  3 us
    pallas_call x1, Pallas kernels, on_device(): pl.pallas_call(functools.partial(second_step, sizes, inline), out_shape=o...  2.62 us
    pallas_call x1, Pallas kernels, on_device(): pl.pallas_call(functools.partial(unpack, where), out_shape=[shape_of(*con...  1.49 us
    pallas_call x1, Pallas kernels, on_device(): pl.pallas_call(pack_faces, out_shape=[shape_of((NF + 1) * chunks, ROWS, l...  1.46 us
  transfers between devices with their start and end apart: 9, of which 2 were waited for; matrix products, arithmetic and copies ran while one was open for 0% of the time, Pallas kernels for 7%

profile of v2, /device:TPU:0, one launch (start us, length us, event | category | flops | bytes accessed | tf_op | source)
XLA Modules:
  0.0 41.5 jit_solution(6207768413162251832)
XLA Ops:
  0.6 0.0 copy-start.1
  0.6 0.0 copy-start
  0.7 1.5 %pack_faces.1 = (f32[20,8,128]{2,1,0:T(8,128)S(1)}, f32[20,8,128]{2,1,0:T(8,128)S(1)}, f32[3,8,128]{2,1,0:T(8,128)S(1)}, f32[10,8,128]{2,1,0:T(8,128)S(1)}, f32[10,8,128]{2,1,0:T(8,128)S(1)}) custom-call(f32[4,8,32,128]{3,2,1,0:T(8,128)} %fields.5, f32[8,32,128]{2,1,0:T(8,128)} %visc.7), custom_call_target="tpu_custom_call" | custom-call | tf_op jit(solution)/shard_map/pack_faces/pallas_call | solution.py:639
  2.1 0.0 copy-start.3
  2.1 2.4 %collective-permute-start = (f32[20,8,128]{2,1,0:T(8,128)S(1)}, f32[20,8,128]{2,1,0:T(8,128)S(1)}, u32[]{:S(2)}, u32[]{:S(2)}) collective-permute-start(f32[20,8,128]{2,1,0:T(8,128)S(1)} %get-tuple-element.35), channel_id=1, source_target_pairs={{0,24},{8,16},{16,8},{24,0},{1,25},{9,17},{17,9},{25,1},{2,26},{10... | collective-permute-start | bytes 245768 | tf_op jit(solution)/shard_map/ppermute | solution.py:610
  4.6 0.7 %collective-permute-start.1 = (f32[20,8,128]{2,1,0:T(8,128)S(1)}, f32[20,8,128]{2,1,0:T(8,128)S(1)}, u32[]{:S(2)}, u32[]{:S(2)}) collective-permute-start(f32[20,8,128]{2,1,0:T(8,128)S(1)} %get-tuple-element.36), channel_id=1, source_target_pairs={{0,8},{8,0},{16,24},{24,16},{1,9},{9,1},{17,25},{25,17},{2,10},{10... | collective-permute-start | bytes 245768 | tf_op jit(solution)/shard_map/ppermute | solution.py:605
  5.2 3.6 %collective-permute-start.3 = (f32[10,8,128]{2,1,0:T(8,128)S(1)}, f32[10,8,128]{2,1,0:T(8,128)S(1)}, u32[]{:S(2)}, u32[]{:S(2)}) collective-permute-start(f32[10,8,128]{2,1,0:T(8,128)S(1)} %get-tuple-element.37), channel_id=1, source_target_pairs={{0,6},{2,4},{4,2},{6,0},{1,7},{3,5},{5,3},{7,1},{8,14},{10,12},{12... | collective-permute-start | bytes 122888 | tf_op jit(solution)/shard_map/ppermute | solution.py:610
  8.9 0.0 collective-permute-start.4
  8.9 0.0 copy-start.4
  8.9 1.5 %collective-permute-start.2 = (f32[3,8,128]{2,1,0:T(8,128)S(1)}, f32[3,8,128]{2,1,0:T(8,128)S(1)}, u32[]{:S(2)}, u32[]{:S(2)}) collective-permute-start(f32[3,8,128]{2,1,0:T(8,128)S(1)} %get-tuple-element.34.z_own.vz_own), channel_id=1, source_target_pairs={{0,1},{1,0},{2,3},{3,2},{4,5},{5,4},{6,7},{7,6},{8,9},{9,8},{10,11... | collective-permute-start | bytes 36872 | tf_op jit(solution)/shard_map/ppermute | solution.py:605
  10.4 0.0 copy-start.5
  10.4 0.0 copy-start.6
  10.4 0.0 copy-done.1
  10.4 0.0 copy-done
  10.4 0.0 copy-done.3
  10.4 0.0 copy-done.4
  10.4 0.6 %copy-done.5 = s32[1,1,1,8]{3,2,1,0:T(1,128)S(1)} copy-done((s32[1,1,1,8]{3,2,1,0:T(1,128)S(1)}, s32[1,1,1,8]{3,2,1,0:T(1,128)}, u32[]{:S(2)}) %copy-start.5) | copy-done | bytes 56
  11.0 0.0 copy-done.6
  11.0 1.5 %interior_first.1 = (f32[4,8,32,128]{3,2,1,0:T(8,128)S(1)}, bf16[32,112]{1,0:T(8,128)(2,1)S(1)}, bf16[16,32]{1,0:T(8,128)(2,1)S(1)}, bf16[32,16]{1,0:T(8,128)(2,1)S(1)}, s32[8,128]{1,0:T(8,128)S(1)}) custom-call(s32[8]{0:T(128)S(1)} %bitcast.2, s32[8]{0:T(128)S(1)} %bitcast.3, f32[4,8,32,128]{3,2,1,0:T(8,128)S(1)} %copy-done, f32[8,32,128]{2,1,0:T(8,128)S(1)} %copy-done.1, ...), custom_call_target="tpu_custom_call" | custom-call | flops 3932160 | bytes 1179648 | tf_op jit(solution)/shard_map/interior_first/pallas_call | solution.py:617
  12.5 0.0 collective-permute-done.2.z_other.vz_other
  12.6 0.0 collective-permute-done.3.y_from_b.y_b.vy_b
  12.6 0.3 collective-permute-done.4.y_from_a.y_a.vy_a
  12.9 0.0 collective-permute-done.x_from_b.vx_b
  12.9 0.0 collective-permute-done.1.x_from_a.vx_a
  12.9 0.0 copy-start.2
  12.9 0.7 %close_first.1 = (f32[4,8,32,128]{3,2,1,0:T(8,128)S(1)}, f32[18,8,128]{2,1,0:T(8,128)S(1)}, f32[9,8,128]{2,1,0:T(8,128)S(1)}, f32[9,8,128]{2,1,0:T(8,128)S(1)}, f32[10,8,128]{2,1,0:T(8,128)S(1)}) custom-call(f32[4,8,32,128]{3,2,1,0:T(8,128)S(1)} %copy-done, f32[8,32,128]{2,1,0:T(8,128)S(1)} %copy-done.1, f32[4,8,32,128]{3,2,1,0:T(8,128)S(1)} %get-tuple-element.33.partial, ...), custom_call_target="tpu_custom_call" | custom-call | tf_op jit(solution)/shard_map/close_first/pallas_call | solution.py:676
  13.5 0.1 collective-permute-start.5
  13.6 1.6 %collective-permute-start.6 = (f32[10,8,128]{2,1,0:T(8,128)S(1)}, f32[10,8,128]{2,1,0:T(8,128)S(1)}, u32[]{:S(2)}, u32[]{:S(2)}) collective-permute-start(f32[10,8,128]{2,1,0:T(8,128)S(1)} %get-tuple-element.42.z_own), channel_id=1, source_target_pairs={{0,1},{1,0},{2,3},{3,2},{4,5},{5,4},{6,7},{7,6},{8,9},{9,8},{10,11... | collective-permute-start | bytes 122888 | tf_op jit(solution)/shard_map/ppermute | solution.py:605
  15.2 0.3 collective-permute-start.7
  15.5 0.2 collective-permute-start.8
  15.7 0.0 copy-done.2
  15.7 1.5 %interior_second.1 = (f32[4,8,32,128]{3,2,1,0:T(8,128)S(1)}, f32[8,8,128]{2,1,0:T(8,128)S(1)}, bf16[864,32]{1,0:T(8,128)(2,1)S(1)}) custom-call(f32[4,8,32,128]{3,2,1,0:T(8,128)S(1)} %get-tuple-element.39.middle, f32[8,32,128]{2,1,0:T(8,128)S(1)} %copy-done.1, f32[4,8,32,128]{3,2,1,0:T(8,128)S(1)} %copy-done, ...), custom_call_target="tpu_custom_call" | custom-call | flops 3932160 | bytes 1179648 | tf_op jit(solution)/shard_map/interior_second/pallas_call | solution.py:617
  17.3 0.0 collective-permute-done.7.x_a_low
  17.3 0.0 collective-permute-done.8.x_a_high
  17.3 0.4 %collective-permute-done.6.z_other = f32[10,8,128]{2,1,0:T(8,128)S(1)} collective-permute-done((f32[10,8,128]{2,1,0:T(8,128)S(1)}, f32[10,8,128]{2,1,0:T(8,128)S(1)}, u32[]{:S(2)}, u32[]{:S(2)}) %collective-permute-start.6) | collective-permute-done | bytes 40992 | tf_op jit(solution)/shard_map/ppermute | solution.py:605
  17.7 0.0 collective-permute-done.5.x_b
  17.7 2.6 %second_step.1 = (f32[4,8,32,128]{3,2,1,0:T(8,128)S(1)}, bf16[32,8,128]{2,1,0:T(8,128)(2,1)S(1)}) custom-call(s32[8,128]{1,0:T(8,128)S(1)} %get-tuple-element.32.drawn, f32[4,8,32,128]{3,2,1,0:T(8,128)S(1)} %get-tuple-element.39.middle, f32[8,32,128]{2,1,0:T(8,128)S(1)} %copy-done.1, f32[4,8,32,128]{3,2,1,0:T(8,128)S(1)} %get-tuple-element.40.partial, ...), custom_call_target="tpu_custom_call" | custom-call | tf_op jit(solution)/shard_map/second_step/pallas_call | solution.py:709
  20.4 10.6 %all_to_all.10.arrived = bf16[32,8,128]{2,1,0:T(8,128)(2,1)S(1)} all-to-all(bf16[32,8,128]{2,1,0:T(8,128)(2,1)S(1)} %get-tuple-element.50), channel_id=1, replica_groups=mesh['gx'=4,'gy'=4,'gz'=2] {'gx','gy','gz'}, dimensions={0} | all-to-all | bytes 131072 | tf_op jit(solution)/shard_map/all_to_all | solution.py:727
  31.0 9.0 %all_to_all.11.gathered = bf16[32,8,128]{2,1,0:T(8,128)(2,1)S(1)} all-to-all(bf16[32,8,128]{2,1,0:T(8,128)(2,1)S(1)} %get-tuple-element.51), channel_id=1, replica_groups=mesh['gx'=4,'gy'=4,'gz'=2] {'gx','gy','gz'}, dimensions={0} | all-to-all | bytes 131072 | tf_op jit(solution)/shard_map/all_to_all | solution.py:742
  40.0 1.5 %unpack.1 = (f32[32,108]{1,0:T(8,128)}, f32[32,864]{1,0:T(8,128)}, f32[6,32]{1,0:T(8,128)}, f32[1,1,1,8]{3,2,1,0:T(1,128)}, f32[4,8,32,128]{3,2,1,0:T(8,128)}) custom-call(bf16[32,8,128]{2,1,0:T(8,128)(2,1)S(1)} %all_to_all.11.gathered, f32[8,128]{1,0:T(8,128)S(1)} %get-tuple-element.52.own, f32[4,8,32,128]{3,2,1,0:T(8,128)S(1)} %get-tuple-element.53.kept), custom_call_target="tpu_custom_call" | custom-call | tf_op jit(solution)/shard_map/unpack/pallas_call | solution.py:743
  (1 shorter events, 0.0 us)
Async XLA Ops:
  0.6 9.8 %copy-start.1 = (f32[8,32,128]{2,1,0:T(8,128)S(1)}, f32[8,32,128]{2,1,0:T(8,128)}, u32[]{:S(2)}) copy-start(f32[8,32,128]{2,1,0:T(8,128)} %visc.7) | copy-start | bytes 393220
  0.6 9.7 %copy-start = (f32[4,8,32,128]{3,2,1,0:T(8,128)S(1)}, f32[4,8,32,128]{3,2,1,0:T(8,128)}, u32[]{:S(2)}) copy-start(f32[4,8,32,128]{3,2,1,0:T(8,128)} %fields.5) | copy-start | bytes 1572868
  2.1 8.3 %copy-start.3 = (bf16[32,108]{1,0:T(8,128)(2,1)S(1)}, bf16[32,108]{1,0:T(8,128)(2,1)}, u32[]{:S(2)}) copy-start(bf16[32,108]{1,0:T(8,128)(2,1)} %conv_first.1) | copy-start | bytes 20740
  2.1 10.7 %collective-permute-start = (f32[20,8,128]{2,1,0:T(8,128)S(1)}, f32[20,8,128]{2,1,0:T(8,128)S(1)}, u32[]{:S(2)}, u32[]{:S(2)}) collective-permute-start(f32[20,8,128]{2,1,0:T(8,128)S(1)} %get-tuple-element.35), channel_id=1, source_target_pairs={{0,24},{8,16},{16,8},{24,0},{1,25},{9,17},{17,9},{25,1},{2,26},{10... | collective-permute-start | bytes 245768 | tf_op jit(solution)/shard_map/ppermute | solution.py:610
  4.6 8.3 %collective-permute-start.1 = (f32[20,8,128]{2,1,0:T(8,128)S(1)}, f32[20,8,128]{2,1,0:T(8,128)S(1)}, u32[]{:S(2)}, u32[]{:S(2)}) collective-permute-start(f32[20,8,128]{2,1,0:T(8,128)S(1)} %get-tuple-element.36), channel_id=1, source_target_pairs={{0,8},{8,0},{16,24},{24,16},{1,9},{9,1},{17,25},{25,17},{2,10},{10... | collective-permute-start | bytes 245768 | tf_op jit(solution)/shard_map/ppermute | solution.py:605
  5.2 7.3 %collective-permute-start.3 = (f32[10,8,128]{2,1,0:T(8,128)S(1)}, f32[10,8,128]{2,1,0:T(8,128)S(1)}, u32[]{:S(2)}, u32[]{:S(2)}) collective-permute-start(f32[10,8,128]{2,1,0:T(8,128)S(1)} %get-tuple-element.37), channel_id=1, source_target_pairs={{0,6},{2,4},{4,2},{6,0},{1,7},{3,5},{5,3},{7,1},{8,14},{10,12},{12... | collective-permute-start | bytes 122888 | tf_op jit(solution)/shard_map/ppermute | solution.py:610
  8.9 4.0 %collective-permute-start.4 = (f32[10,8,128]{2,1,0:T(8,128)S(1)}, f32[10,8,128]{2,1,0:T(8,128)S(1)}, u32[]{:S(2)}, u32[]{:S(2)}) collective-permute-start(f32[10,8,128]{2,1,0:T(8,128)S(1)} %get-tuple-element.38), channel_id=1, source_target_pairs={{0,2},{2,0},{4,6},{6,4},{1,3},{3,1},{5,7},{7,5},{8,10},{10,8},{12,... | collective-permute-start | bytes 122888 | tf_op jit(solution)/shard_map/ppermute | solution.py:605
  8.9 1.5 %copy-start.4 = (bf16[6,32]{1,0:T(8,128)(2,1)S(1)}, bf16[6,32]{1,0:T(8,128)(2,1)}, u32[]{:S(2)}) copy-start(bf16[6,32]{1,0:T(8,128)(2,1)} %conv_third.1) | copy-start | bytes 1156
  8.9 3.7 %collective-permute-start.2 = (f32[3,8,128]{2,1,0:T(8,128)S(1)}, f32[3,8,128]{2,1,0:T(8,128)S(1)}, u32[]{:S(2)}, u32[]{:S(2)}) collective-permute-start(f32[3,8,128]{2,1,0:T(8,128)S(1)} %get-tuple-element.34.z_own.vz_own), channel_id=1, source_target_pairs={{0,1},{1,0},{2,3},{3,2},{4,5},{5,4},{6,7},{7,6},{8,9},{9,8},{10,11... | collective-permute-start | bytes 36872 | tf_op jit(solution)/shard_map/ppermute | solution.py:605
  10.4 0.7 %copy-start.5 = (s32[1,1,1,8]{3,2,1,0:T(1,128)S(1)}, s32[1,1,1,8]{3,2,1,0:T(1,128)}, u32[]{:S(2)}) copy-start(s32[1,1,1,8]{3,2,1,0:T(1,128)} %param.9) | copy-start | bytes 100
  10.4 0.7 %copy-start.6 = (s32[1,1,1,8,1]{3,4,2,1,0:T(1,128)S(1)}, s32[1,1,1,8,1]{3,4,2,1,0:T(1,128)}, u32[]{:S(2)}) copy-start(s32[1,1,1,8,1]{3,4,2,1,0:T(1,128)} %param.10) | copy-start | bytes 100
  12.9 2.9 %copy-start.2 = (bf16[32,864]{1,0:T(8,128)(2,1)S(1)}, bf16[32,864]{1,0:T(8,128)(2,1)}, u32[]{:S(2)}) copy-start(bf16[32,864]{1,0:T(8,128)(2,1)} %rest_1_.1) | copy-start | bytes 165892
  13.5 4.2 %collective-permute-start.5 = (f32[18,8,128]{2,1,0:T(8,128)S(1)}, f32[18,8,128]{2,1,0:T(8,128)S(1)}, u32[]{:S(2)}, u32[]{:S(2)}) collective-permute-start(f32[18,8,128]{2,1,0:T(8,128)S(1)} %get-tuple-element.43), channel_id=1, source_target_pairs={{0,24},{8,16},{16,8},{24,0},{1,25},{9,17},{17,9},{25,1},{2,26},{10... | collective-permute-start | bytes 221192 | tf_op jit(solution)/shard_map/ppermute | solution.py:610
  13.6 4.1 %collective-permute-start.6 = (f32[10,8,128]{2,1,0:T(8,128)S(1)}, f32[10,8,128]{2,1,0:T(8,128)S(1)}, u32[]{:S(2)}, u32[]{:S(2)}) collective-permute-start(f32[10,8,128]{2,1,0:T(8,128)S(1)} %get-tuple-element.42.z_own), channel_id=1, source_target_pairs={{0,1},{1,0},{2,3},{3,2},{4,5},{5,4},{6,7},{7,6},{8,9},{9,8},{10,11... | collective-permute-start | bytes 122888 | tf_op jit(solution)/shard_map/ppermute | solution.py:605
  15.2 2.1 %collective-permute-start.7 = (f32[9,8,128]{2,1,0:T(8,128)S(1)}, f32[9,8,128]{2,1,0:T(8,128)S(1)}, u32[]{:S(2)}, u32[]{:S(2)}) collective-permute-start(f32[9,8,128]{2,1,0:T(8,128)S(1)} %get-tuple-element.44), channel_id=1, source_target_pairs={{0,8},{8,0},{16,24},{24,16},{1,9},{9,1},{17,25},{25,17},{2,10},{10... | collective-permute-start | bytes 110600 | tf_op jit(solution)/shard_map/ppermute | solution.py:605
  15.5 1.8 %collective-permute-start.8 = (f32[9,8,128]{2,1,0:T(8,128)S(1)}, f32[9,8,128]{2,1,0:T(8,128)S(1)}, u32[]{:S(2)}, u32[]{:S(2)}) collective-permute-start(f32[9,8,128]{2,1,0:T(8,128)S(1)} %get-tuple-element.45), channel_id=1, source_target_pairs={{0,8},{8,0},{16,24},{24,16},{1,9},{9,1},{17,25},{25,17},{2,10},{10... | collective-permute-start | bytes 110600 | tf_op jit(solution)/shard_map/ppermute | solution.py:605

commit v3 on v1

--- a/solution.py
+++ b/solution.py
@@ -329,8 +329,8 @@
 
 
 def close_first(fields, visc, partial, z_own, x_from_b, x_from_a, z_other, y_from_b, y_from_a,
-                middle, x_b, x_a_low, x_a_high, z_both, y_terms):
-    x_a = Parts(x_a_low, x_a_high)
+                middle, x_b, x_a_low, x_a_mid, x_a_high, z_both, y_terms):
+    x_a = Parts(x_a_low, x_a_mid, x_a_high)
     _, planes, rows, _ = fields.shape
     chunks = rows // ROWS
     halo = Sides(chunks, x_from_b, x_from_a, z_other, y_from_b, y_from_a)
@@ -545,13 +545,13 @@
 
 
 def second_step(sizes, inline, drawn, middle, visc, partial, rims, vz_own, vx_b, vx_a, vz_other, vy_b, vy_a,
-                z_own, x_b, z_other, x_a_low, x_a_high, *rest):
+                z_own, x_b, z_other, x_a_low, x_a_mid, x_a_high, *rest):
     loads, rest = (None, rest) if sizes["gy"] * CAP == SAMP else (rest[0][...], rest[1:])
     w_first, w_second, w_second_t, w_third, w_third_t, advanced_far, send = rest[:7]
     slots = None if inline else rest[7]
     stack_first, stack_mid, rows_out, y_terms, advanced, sem = rest[-6:]
     chunks = middle.shape[2] // ROWS
-    halo = Sides(chunks, x_b, Parts(x_a_low, x_a_high), z_other)
+    halo = Sides(chunks, x_b, Parts(x_a_low, x_a_mid, x_a_high), z_other)
     visc_halo = Sides(chunks, vx_b, vx_a, vz_other, vy_b, vy_a)
     y_faces = rims_with_ends(rims, visc_halo, halo)
     y_faces = [face + [visc_halo.along_y(NF)[side]] for side, face in enumerate(y_faces)]
@@ -673,24 +673,23 @@
         (samples, trainers), (fields, visc, conv_first, conv_third),
     )
     y_terms = pltpu.VMEM((2, NF, planes, lanes), jnp.float32)
-    middle, x_b, x_a_low, x_a_high, z_later = pl.pallas_call(
+    middle, x_b, x_a_low, x_a_mid, x_a_high, z_later = pl.pallas_call(
         close_first,
         out_shape=[
             shape_of(*fields.shape),
             shape_of(NF * chunks + 2, ROWS, lanes),
-            shape_of(NF * chunks // 2 + 1, ROWS, lanes),
-            shape_of(NF * chunks // 2 + 1, ROWS, lanes),
-            shape_of(NF * chunks // 2 + 2, ROWS, LANES),
+            *[shape_of((NF * chunks + 2) // 3, ROWS, lanes)] * 3,
+            shape_of((NF * chunks + 2) // 3 + 1, ROWS, LANES),
         ],
         in_specs=[VMEM] * 9,
-        out_specs=[VMEM] * 5,
+        out_specs=[VMEM] * 6,
         scratch_shapes=[y_terms],
         compiler_params=PARAMS,
         name="close_first",
     )(fields, visc, partial, z_own, *halo)
     later = [
         swap_b(x_b, "gx", sizes), swap_a(z_later, "gz", sizes),
-        swap_a(x_a_low, "gx", sizes), swap_a(x_a_high, "gx", sizes),
+        swap_a(x_a_low, "gx", sizes), swap_a(x_a_mid, "gx", sizes), swap_a(x_a_high, "gx", sizes),
     ]
     partial, rims, w_second_t = beside(
         interior_second, visc.size,
@@ -709,7 +708,7 @@
     advanced, send, *slots = pl.pallas_call(
         functools.partial(second_step, sizes, inline),
         out_shape=out_shape,
-        in_specs=[VMEM] * (21 + len(counts)),
+        in_specs=[VMEM] * (22 + len(counts)),
         out_specs=[ANY] + [VMEM] * (len(out_shape) - 1),
         scratch_shapes=[
             pltpu.VMEM((28 * NF, count * VOL), jnp.float32),

time: 41.4 us -> 41.5 us (level)
  waiting for transfers between devices: 0.79 us -> 0.36 us
    ppermute x6 -> x7, waiting for transfers between devices: 0.78 us -> 0.35 us  [swap_a(): return lax.ppermute(face, axis, [(i, i ^ 1) for i in range(sizes[axis])])]
    ppermute x6 -> x7, starting transfers between devices: 4.29 us -> 4.58 us  [swap_a(): return lax.ppermute(face, axis, [(i, i ^ 1) for i in range(sizes[axis])])]
  transfers between devices with their start and end apart: 9 -> 10, of which waited for: 2 -> 1; matrix products, arithmetic and copies ran while one was open for 0% -> 0% of each run, Pallas kernels for 7% -> 7%
where the time goes in v3:
time: 41.5 us; the launch traced here: 41.3 us
  blocking collectives  19.7 us (47%)
  starting transfers between devices  10.7 us (26%)
  Pallas kernels  9.11 us (22%)
  between operations  0.77 us (2%)
  local copies, waits for them, and re-layouts  0.66 us (2%)
    all_to_all x1, blocking collectives, on_device(): lax.all_to_all(send, axes, split_axis=0, concat_axis=0, tiled=True)  10.7 us
    all_to_all x1, blocking collectives, on_device(): lax.all_to_all(spread, axes, split_axis=0, concat_axis=0, tiled=True)  8.97 us
    ppermute x3, starting transfers between devices, swap_b(): lax.ppermute(face, axis, [(i, (i + (1 if i % 2 else -1)) % count) for i i...  6.12 us
    ppermute x7, starting transfers between devices, swap_a(): return lax.ppermute(face, axis, [(i, i ^ 1) for i in range(sizes[axis])])  4.58 us
    pallas_call x1, Pallas kernels, on_device(): pl.pallas_call(functools.partial(second_step, sizes, inline), out_shape=o...  3.12 us
    pallas_call x2, Pallas kernels, beside(): pl.pallas_call(kernel, out_shape=[shape_of(*arrays[0].shape)] + more_shap...  3.01 us
    pallas_call x1, Pallas kernels, on_device(): pl.pallas_call(pack_faces, out_shape=[shape_of((NF + 1) * chunks, ROWS, l...  1.46 us
  transfers between devices with their start and end apart: 10, of which 1 were waited for; matrix products, arithmetic and copies ran while one was open for 0% of the time, Pallas kernels for 7%

profile of v3, /device:TPU:0, one launch (start us, length us, event | category | flops | bytes accessed | tf_op | source)
XLA Modules:
  0.0 41.3 jit_solution(10990212143947172931)
XLA Ops:
  0.6 0.0 copy-start.1
  0.6 0.0 copy-start
  0.7 1.5 %pack_faces.1 = (f32[20,8,128]{2,1,0:T(8,128)S(1)}, f32[20,8,128]{2,1,0:T(8,128)S(1)}, f32[3,8,128]{2,1,0:T(8,128)S(1)}, f32[10,8,128]{2,1,0:T(8,128)S(1)}, f32[10,8,128]{2,1,0:T(8,128)S(1)}) custom-call(f32[4,8,32,128]{3,2,1,0:T(8,128)} %fields.5, f32[8,32,128]{2,1,0:T(8,128)} %visc.7), custom_call_target="tpu_custom_call" | custom-call | tf_op jit(solution)/shard_map/pack_faces/pallas_call | solution.py:639
  2.1 0.0 copy-start.3
  2.1 2.4 %collective-permute-start = (f32[20,8,128]{2,1,0:T(8,128)S(1)}, f32[20,8,128]{2,1,0:T(8,128)S(1)}, u32[]{:S(2)}, u32[]{:S(2)}) collective-permute-start(f32[20,8,128]{2,1,0:T(8,128)S(1)} %get-tuple-element.35), channel_id=1, source_target_pairs={{0,24},{8,16},{16,8},{24,0},{1,25},{9,17},{17,9},{25,1},{2,26},{10... | collective-permute-start | bytes 245768 | tf_op jit(solution)/shard_map/ppermute | solution.py:610
  4.6 0.7 %collective-permute-start.1 = (f32[20,8,128]{2,1,0:T(8,128)S(1)}, f32[20,8,128]{2,1,0:T(8,128)S(1)}, u32[]{:S(2)}, u32[]{:S(2)}) collective-permute-start(f32[20,8,128]{2,1,0:T(8,128)S(1)} %get-tuple-element.36), channel_id=1, source_target_pairs={{0,8},{8,0},{16,24},{24,16},{1,9},{9,1},{17,25},{25,17},{2,10},{10... | collective-permute-start | bytes 245768 | tf_op jit(solution)/shard_map/ppermute | solution.py:605
  5.2 3.6 %collective-permute-start.3 = (f32[10,8,128]{2,1,0:T(8,128)S(1)}, f32[10,8,128]{2,1,0:T(8,128)S(1)}, u32[]{:S(2)}, u32[]{:S(2)}) collective-permute-start(f32[10,8,128]{2,1,0:T(8,128)S(1)} %get-tuple-element.37), channel_id=1, source_target_pairs={{0,6},{2,4},{4,2},{6,0},{1,7},{3,5},{5,3},{7,1},{8,14},{10,12},{12... | collective-permute-start | bytes 122888 | tf_op jit(solution)/shard_map/ppermute | solution.py:610
  8.9 0.0 collective-permute-start.4
  8.9 0.0 copy-start.4
  8.9 1.5 %collective-permute-start.2 = (f32[3,8,128]{2,1,0:T(8,128)S(1)}, f32[3,8,128]{2,1,0:T(8,128)S(1)}, u32[]{:S(2)}, u32[]{:S(2)}) collective-permute-start(f32[3,8,128]{2,1,0:T(8,128)S(1)} %get-tuple-element.34.z_own.vz_own), channel_id=1, source_target_pairs={{0,1},{1,0},{2,3},{3,2},{4,5},{5,4},{6,7},{7,6},{8,9},{9,8},{10,11... | collective-permute-start | bytes 36872 | tf_op jit(solution)/shard_map/ppermute | solution.py:605
  10.4 0.0 copy-start.5
  10.4 0.0 copy-start.6
  10.4 0.0 copy-done.1
  10.4 0.0 copy-done
  10.4 0.0 copy-done.3
  10.4 0.0 copy-done.4
  10.4 0.6 %copy-done.5 = s32[1,1,1,8]{3,2,1,0:T(1,128)S(1)} copy-done((s32[1,1,1,8]{3,2,1,0:T(1,128)S(1)}, s32[1,1,1,8]{3,2,1,0:T(1,128)}, u32[]{:S(2)}) %copy-start.5) | copy-done | bytes 56
  11.0 0.0 copy-done.6
  11.0 1.5 %interior_first.1 = (f32[4,8,32,128]{3,2,1,0:T(8,128)S(1)}, bf16[32,112]{1,0:T(8,128)(2,1)S(1)}, bf16[16,32]{1,0:T(8,128)(2,1)S(1)}, bf16[32,16]{1,0:T(8,128)(2,1)S(1)}, s32[8,128]{1,0:T(8,128)S(1)}) custom-call(s32[8]{0:T(128)S(1)} %bitcast.2, s32[8]{0:T(128)S(1)} %bitcast.3, f32[4,8,32,128]{3,2,1,0:T(8,128)S(1)} %copy-done, f32[8,32,128]{2,1,0:T(8,128)S(1)} %copy-done.1, ...), custom_call_target="tpu_custom_call" | custom-call | flops 3932160 | bytes 1179648 | tf_op jit(solution)/shard_map/interior_first/pallas_call | solution.py:617
  12.5 0.0 collective-permute-done.2.z_other.vz_other
  12.6 0.0 collective-permute-done.3.y_from_b.y_b.vy_b
  12.6 0.3 collective-permute-done.4.y_from_a.y_a.vy_a
  12.9 0.0 collective-permute-done.x_from_b.vx_b
  12.9 0.0 collective-permute-done.1.x_from_a.vx_a
  12.9 0.0 copy-start.2
  12.9 0.7 %close_first.1 = (f32[4,8,32,128]{3,2,1,0:T(8,128)S(1)}, f32[18,8,128]{2,1,0:T(8,128)S(1)}, f32[6,8,128]{2,1,0:T(8,128)S(1)}, f32[6,8,128]{2,1,0:T(8,128)S(1)}, ...) custom-call(f32[4,8,32,128]{3,2,1,0:T(8,128)S(1)} %copy-done, f32[8,32,128]{2,1,0:T(8,128)S(1)} %copy-done.1, ...), custom_call_target="tpu_custom_call" | custom-call | tf_op jit(solution)/shard_map/close_first/pallas_call | solution.py:676
  13.6 0.1 collective-permute-start.5
  13.6 1.6 %collective-permute-start.6 = (f32[7,8,128]{2,1,0:T(8,128)S(1)}, f32[7,8,128]{2,1,0:T(8,128)S(1)}, u32[]{:S(2)}, u32[]{:S(2)}) collective-permute-start(f32[7,8,128]{2,1,0:T(8,128)S(1)} %get-tuple-element.42.z_own), channel_id=1, source_target_pairs={{0,1},{1,0},{2,3},{3,2},{4,5},{5,4},{6,7},{7,6},{8,9},{9,8},{10,11... | collective-permute-start | bytes 86024 | tf_op jit(solution)/shard_map/ppermute | solution.py:605
  15.2 0.3 collective-permute-start.7
  15.5 0.2 collective-permute-start.8
  15.7 0.3 collective-permute-start.9
  16.0 0.0 copy-done.2
  16.0 1.5 %interior_second.1 = (f32[4,8,32,128]{3,2,1,0:T(8,128)S(1)}, f32[8,8,128]{2,1,0:T(8,128)S(1)}, bf16[864,32]{1,0:T(8,128)(2,1)S(1)}) custom-call(f32[4,8,32,128]{3,2,1,0:T(8,128)S(1)} %get-tuple-element.39.middle, f32[8,32,128]{2,1,0:T(8,128)S(1)} %copy-done.1, f32[4,8,32,128]{3,2,1,0:T(8,128)S(1)} %copy-done, ...), custom_call_target="tpu_custom_call" | custom-call | flops 3932160 | bytes 1179648 | tf_op jit(solution)/shard_map/interior_second/pallas_call | solution.py:617
  17.6 0.0 collective-permute-done.7.x_a_low
  17.6 0.0 collective-permute-done.8.x_a_mid
  17.6 0.0 collective-permute-done.9.x_a_high
  17.6 0.0 collective-permute-done.6.z_other
  17.6 0.0 collective-permute-done.5.x_b
  17.6 3.1 %second_step.1 = (f32[4,8,32,128]{3,2,1,0:T(8,128)}, bf16[32,8,128]{2,1,0:T(8,128)(2,1)S(1)}) custom-call(s32[8,128]{1,0:T(8,128)S(1)} %get-tuple-element.32.drawn, f32[4,8,32,128]{3,2,1,0:T(8,128)S(1)} %get-tuple-element.39.middle, f32[8,32,128]{2,1,0:T(8,128)S(1)} %copy-done.1, f32[4,8,32,128]{3,2,1,0:T(8,128)S(1)} %get-tuple-element.40.partial, ...), custom_call_target="tpu_custom_call" | custom-call | tf_op jit(solution)/shard_map/second_step/pallas_call | solution.py:708
  20.8 10.7 %all_to_all.10.arrived = bf16[32,8,128]{2,1,0:T(8,128)(2,1)S(1)} all-to-all(bf16[32,8,128]{2,1,0:T(8,128)(2,1)S(1)} %get-tuple-element.52), channel_id=1, replica_groups=mesh['gx'=4,'gy'=4,'gz'=2] {'gx','gy','gz'}, dimensions={0} | all-to-all | bytes 131072 | tf_op jit(solution)/shard_map/all_to_all | solution.py:728
  31.5 9.0 %all_to_all.11.gathered = bf16[32,8,128]{2,1,0:T(8,128)(2,1)S(1)} all-to-all(bf16[32,8,128]{2,1,0:T(8,128)(2,1)S(1)} %get-tuple-element.53), channel_id=1, replica_groups=mesh['gx'=4,'gy'=4,'gz'=2] {'gx','gy','gz'}, dimensions={0} | all-to-all | bytes 131072 | tf_op jit(solution)/shard_map/all_to_all | solution.py:743
  40.5 0.8 %unpack.1 = (f32[32,108]{1,0:T(8,128)}, f32[32,864]{1,0:T(8,128)}, f32[6,32]{1,0:T(8,128)}, f32[1,1,1,8]{3,2,1,0:T(1,128)}) custom-call(bf16[32,8,128]{2,1,0:T(8,128)(2,1)S(1)} %all_to_all.11.gathered, f32[8,128]{1,0:T(8,128)S(1)} %get-tuple-element.54.own), custom_call_target="tpu_custom_call" | custom-call | tf_op jit(solution)/shard_map/unpack/pallas_call | solution.py:744
  (1 shorter events, 0.0 us)
Async XLA Ops:
  0.6 9.8 %copy-start.1 = (f32[8,32,128]{2,1,0:T(8,128)S(1)}, f32[8,32,128]{2,1,0:T(8,128)}, u32[]{:S(2)}) copy-start(f32[8,32,128]{2,1,0:T(8,128)} %visc.7) | copy-start | bytes 393220
  0.6 9.7 %copy-start = (f32[4,8,32,128]{3,2,1,0:T(8,128)S(1)}, f32[4,8,32,128]{3,2,1,0:T(8,128)}, u32[]{:S(2)}) copy-start(f32[4,8,32,128]{3,2,1,0:T(8,128)} %fields.5) | copy-start | bytes 1572868
  2.1 8.3 %copy-start.3 = (bf16[32,108]{1,0:T(8,128)(2,1)S(1)}, bf16[32,108]{1,0:T(8,128)(2,1)}, u32[]{:S(2)}) copy-start(bf16[32,108]{1,0:T(8,128)(2,1)} %conv_first.1) | copy-start | bytes 20740
  2.1 10.7 %collective-permute-start = (f32[20,8,128]{2,1,0:T(8,128)S(1)}, f32[20,8,128]{2,1,0:T(8,128)S(1)}, u32[]{:S(2)}, u32[]{:S(2)}) collective-permute-start(f32[20,8,128]{2,1,0:T(8,128)S(1)} %get-tuple-element.35), channel_id=1, source_target_pairs={{0,24},{8,16},{16,8},{24,0},{1,25},{9,17},{17,9},{25,1},{2,26},{10... | collective-permute-start | bytes 245768 | tf_op jit(solution)/shard_map/ppermute | solution.py:610
  4.6 8.3 %collective-permute-start.1 = (f32[20,8,128]{2,1,0:T(8,128)S(1)}, f32[20,8,128]{2,1,0:T(8,128)S(1)}, u32[]{:S(2)}, u32[]{:S(2)}) collective-permute-start(f32[20,8,128]{2,1,0:T(8,128)S(1)} %get-tuple-element.36), channel_id=1, source_target_pairs={{0,8},{8,0},{16,24},{24,16},{1,9},{9,1},{17,25},{25,17},{2,10},{10... | collective-permute-start | bytes 245768 | tf_op jit(solution)/shard_map/ppermute | solution.py:605
  5.2 7.3 %collective-permute-start.3 = (f32[10,8,128]{2,1,0:T(8,128)S(1)}, f32[10,8,128]{2,1,0:T(8,128)S(1)}, u32[]{:S(2)}, u32[]{:S(2)}) collective-permute-start(f32[10,8,128]{2,1,0:T(8,128)S(1)} %get-tuple-element.37), channel_id=1, source_target_pairs={{0,6},{2,4},{4,2},{6,0},{1,7},{3,5},{5,3},{7,1},{8,14},{10,12},{12... | collective-permute-start | bytes 122888 | tf_op jit(solution)/shard_map/ppermute | solution.py:610
  8.9 4.0 %collective-permute-start.4 = (f32[10,8,128]{2,1,0:T(8,128)S(1)}, f32[10,8,128]{2,1,0:T(8,128)S(1)}, u32[]{:S(2)}, u32[]{:S(2)}) collective-permute-start(f32[10,8,128]{2,1,0:T(8,128)S(1)} %get-tuple-element.38), channel_id=1, source_target_pairs={{0,2},{2,0},{4,6},{6,4},{1,3},{3,1},{5,7},{7,5},{8,10},{10,8},{12,... | collective-permute-start | bytes 122888 | tf_op jit(solution)/shard_map/ppermute | solution.py:605
  8.9 1.5 %copy-start.4 = (bf16[6,32]{1,0:T(8,128)(2,1)S(1)}, bf16[6,32]{1,0:T(8,128)(2,1)}, u32[]{:S(2)}) copy-start(bf16[6,32]{1,0:T(8,128)(2,1)} %conv_third.1) | copy-start | bytes 1156
  8.9 3.7 %collective-permute-start.2 = (f32[3,8,128]{2,1,0:T(8,128)S(1)}, f32[3,8,128]{2,1,0:T(8,128)S(1)}, u32[]{:S(2)}, u32[]{:S(2)}) collective-permute-start(f32[3,8,128]{2,1,0:T(8,128)S(1)} %get-tuple-element.34.z_own.vz_own), channel_id=1, source_target_pairs={{0,1},{1,0},{2,3},{3,2},{4,5},{5,4},{6,7},{7,6},{8,9},{9,8},{10,11... | collective-permute-start | bytes 36872 | tf_op jit(solution)/shard_map/ppermute | solution.py:605
  10.4 0.7 %copy-start.5 = (s32[1,1,1,8]{3,2,1,0:T(1,128)S(1)}, s32[1,1,1,8]{3,2,1,0:T(1,128)}, u32[]{:S(2)}) copy-start(s32[1,1,1,8]{3,2,1,0:T(1,128)} %param.9) | copy-start | bytes 100
  10.4 0.7 %copy-start.6 = (s32[1,1,1,8,1]{3,4,2,1,0:T(1,128)S(1)}, s32[1,1,1,8,1]{3,4,2,1,0:T(1,128)}, u32[]{:S(2)}) copy-start(s32[1,1,1,8,1]{3,4,2,1,0:T(1,128)} %param.10) | copy-start | bytes 100
  12.9 3.2 %copy-start.2 = (bf16[32,864]{1,0:T(8,128)(2,1)S(1)}, bf16[32,864]{1,0:T(8,128)(2,1)}, u32[]{:S(2)}) copy-start(bf16[32,864]{1,0:T(8,128)(2,1)} %rest_1_.1) | copy-start | bytes 165892
  13.6 4.1 %collective-permute-start.5 = (f32[18,8,128]{2,1,0:T(8,128)S(1)}, f32[18,8,128]{2,1,0:T(8,128)S(1)}, u32[]{:S(2)}, u32[]{:S(2)}) collective-permute-start(f32[18,8,128]{2,1,0:T(8,128)S(1)} %get-tuple-element.43), channel_id=1, source_target_pairs={{0,24},{8,16},{16,8},{24,0},{1,25},{9,17},{17,9},{25,1},{2,26},{10... | collective-permute-start | bytes 221192 | tf_op jit(solution)/shard_map/ppermute | solution.py:610
  13.6 4.0 %collective-permute-start.6 = (f32[7,8,128]{2,1,0:T(8,128)S(1)}, f32[7,8,128]{2,1,0:T(8,128)S(1)}, u32[]{:S(2)}, u32[]{:S(2)}) collective-permute-start(f32[7,8,128]{2,1,0:T(8,128)S(1)} %get-tuple-element.42.z_own), channel_id=1, source_target_pairs={{0,1},{1,0},{2,3},{3,2},{4,5},{5,4},{6,7},{7,6},{8,9},{9,8},{10,11... | collective-permute-start | bytes 86024 | tf_op jit(solution)/shard_map/ppermute | solution.py:605
  15.2 2.4 %collective-permute-start.7 = (f32[6,8,128]{2,1,0:T(8,128)S(1)}, f32[6,8,128]{2,1,0:T(8,128)S(1)}, u32[]{:S(2)}, u32[]{:S(2)}) collective-permute-start(f32[6,8,128]{2,1,0:T(8,128)S(1)} %get-tuple-element.44), channel_id=1, source_target_pairs={{0,8},{8,0},{16,24},{24,16},{1,9},{9,1},{17,25},{25,17},{2,10},{10... | collective-permute-start | bytes 73736 | tf_op jit(solution)/shard_map/ppermute | solution.py:605
  15.5 2.1 %collective-permute-start.8 = (f32[6,8,128]{2,1,0:T(8,128)S(1)}, f32[6,8,128]{2,1,0:T(8,128)S(1)}, u32[]{:S(2)}, u32[]{:S(2)}) collective-permute-start(f32[6,8,128]{2,1,0:T(8,128)S(1)} %get-tuple-element.45), channel_id=1, source_target_pairs={{0,8},{8,0},{16,24},{24,16},{1,9},{9,1},{17,25},{25,17},{2,10},{10... | collective-permute-start | bytes 73736 | tf_op jit(solution)/shard_map/ppermute | solution.py:605
  15.7 1.9 %collective-permute-start.9 = (f32[6,8,128]{2,1,0:T(8,128)S(1)}, f32[6,8,128]{2,1,0:T(8,128)S(1)}, u32[]{:S(2)}, u32[]{:S(2)}) collective-permute-start(f32[6,8,128]{2,1,0:T(8,128)S(1)} %get-tuple-element.46), channel_id=1, source_target_pairs={{0,8},{8,0},{16,24},{24,16},{1,9},{9,1},{17,25},{25,17},{2,10},{10... | collective-permute-start | bytes 73736 | tf_op jit(solution)/shard_map/ppermute | solution.py:605
